TPU v7x, 512 devices: a whole 4x8x8 slice. The times are simulated.
512 devices in a mesh: dp: 32 (over z_hi, y, core), mp: 16 (over z_lo, x).
Axes of the slice: x: 4, y: 8, z: 8 (z_hi: 2, z_lo: 4; z = z_hi * 4 + z_lo), core: 2. Of those that a mesh axis runs over, the one named last changes fastest.
Arguments:
- tokens: bfloat16 [256, 8192], P('mp', 'dp'), may hold values from -6 to 6
- gate_weight: bfloat16 [8192, 14336], P('dp', 'mp'), may hold values from -0.0625 to 0.0625
- up_weight: bfloat16 [8192, 14336], P('dp', 'mp'), may hold values from -0.0625 to 0.0625
- down_weight: bfloat16 [14336, 8192], P('mp', 'dp'), may hold values from -0.046875 to 0.046875
- cotangent: bfloat16 [256, 8192], P('mp', 'dp'), may hold values from -6 to 6
Outputs:
- output: bfloat16 [256, 8192], P('mp', 'dp')
- tokens_grad: bfloat16 [256, 8192], P('mp', 'dp')
- gate_grad: bfloat16 [8192, 14336], P('dp', 'mp')
- up_grad: bfloat16 [8192, 14336], P('dp', 'mp')
- down_grad: bfloat16 [14336, 8192], P('mp', 'dp')
All inputs are finite; a program needn't handle non-finite values.
Results may differ from a plain program's by a relative error of at most 0.0049.
Values may be sent and summed in bfloat16 or wider, within the bound.
A program may use at most 64 MiB of HBM per device.

v0:
```python
import math

import jax
import jax.numpy as jnp
from jax import lax
from jax.sharding import PartitionSpec as P


def contract_last(left_side, right_side):
    return lax.dot_general(
        left_side, right_side, (((1,), (1,)), ((), ())), preferred_element_type=jnp.float32
    )


def contract_first(left_side, right_side):
    return lax.dot_general(
        left_side, right_side, (((0,), (0,)), ((), ())), preferred_element_type=jnp.float32
    )


def gating_grads(grad_hidden, gate_sum, up_sum, sigmoid_gate):
    grad_gate = (
        grad_hidden * up_sum * sigmoid_gate * (1.0 + gate_sum * (1.0 - sigmoid_gate))
    ).astype(jnp.bfloat16)
    grad_up = (grad_hidden * gate_sum * sigmoid_gate).astype(jnp.bfloat16)
    return (grad_gate, grad_up)


def on_device(tokens, gate_weight, up_weight, down_weight, cotangent):
    row_count = tokens.shape[0]
    token_count = row_count * lax.axis_size("mp")
    factor = 1.0 / math.sqrt(token_count)
    gathered = lax.all_gather(tokens, "mp", axis=0, tiled=True)
    gate_part = jnp.dot(gathered, gate_weight, preferred_element_type=jnp.float32)
    up_part = jnp.dot(gathered, up_weight, preferred_element_type=jnp.float32)
    grad_output = lax.all_gather(cotangent, "mp", axis=0, tiled=True)
    hidden_part = contract_last(grad_output, down_weight)
    gate_sum, up_sum = lax.psum((gate_part, up_part), "dp")
    sigmoid_gate = jax.nn.sigmoid(gate_sum)
    hidden = (gate_sum * sigmoid_gate * up_sum).astype(jnp.bfloat16)
    grad_hidden = lax.psum(hidden_part, "dp")
    grad_gate, grad_up = gating_grads(grad_hidden, gate_sum, up_sum, sigmoid_gate)
    output = lax.psum_scatter(
        jnp.dot(hidden, down_weight, preferred_element_type=jnp.float32),
        "mp",
        scatter_dimension=0,
        tiled=True,
    ).astype(jnp.bfloat16)
    tokens_grad = lax.psum_scatter(
        contract_last(grad_gate, gate_weight) + contract_last(grad_up, up_weight),
        "mp",
        scatter_dimension=0,
        tiled=True,
    ).astype(jnp.bfloat16)
    gate_grad = (contract_first(gathered, grad_gate) * factor).astype(jnp.bfloat16)
    up_grad = (contract_first(gathered, grad_up) * factor).astype(jnp.bfloat16)
    down_grad = (contract_first(hidden, grad_output) * factor).astype(jnp.bfloat16)
    return (output, tokens_grad, gate_grad, up_grad, down_grad)


def solution(mesh):
    in_specs = (P("mp", "dp"), P("dp", "mp"), P("dp", "mp"), P("mp", "dp"), P("mp", "dp"))
    out_specs = (P("mp", "dp"), P("mp", "dp"), P("dp", "mp"), P("dp", "mp"), P("mp", "dp"))
    return jax.shard_map(
        on_device, mesh=mesh, in_specs=in_specs, out_specs=out_specs, check_vma=False
    )
```

profile of v0, /device:TPU:1, one launch (start us, length us, event | category | flops | bytes accessed | tf_op | source)
XLA Modules:
  0.0 619.2 jit_solution(17767639080887701381)
XLA Ops:
  7.2 0.0 copy-start
  7.2 0.0 copy-start.3
  7.2 0.0 all-reduce.3.cloned.1.call-start
  7.2 39.5 %all_gather.6 = bf16[256,256]{1,0:T(8,128)(2,1)S(1)} all-gather(bf16[16,256]{1,0:T(8,128)(2,1)} %param.5), channel_id=1, replica_groups=mesh['dp'=32,'mp'=16] {'mp'}, dimensions={0}, use_global_device_ids=true | all-gather | bytes 139264 | tf_op jit(solution)/shard_map/all_gather | solution.py:33
  46.8 0.0 copy-done.3
  46.8 30.6 %all_gather.7 = bf16[256,256]{1,0:T(8,128)(2,1)S(1)} all-gather(bf16[16,256]{1,0:T(8,128)(2,1)S(1)} %copy-done.3), channel_id=1, replica_groups=mesh['dp'=32,'mp'=16] {'mp'}, dimensions={0}, use_global_device_ids=true | all-gather | bytes 139264 | tf_op jit(solution)/shard_map/all_gather | solution.py:36
  77.4 2.2 fusion.6
  79.6 0.0 copy-done
  79.6 0.0 copy-start.1
  79.6 1.2 fusion.5
  80.8 0.0 copy-done.1
  80.8 1.3 fusion.8
  82.1 0.0 all-reduce.3.cloned.1.call-update
  82.2 0.0 reduce-scatter.5.cloned.1.call-start
  82.2 364.1 %all-reduce.3.cloned.1.call-done = (f32[256,896]{1,0:T(8,128)}, f32[256,896]{1,0:T(8,128)}, f32[256,896]{1,0:T(8,128)}) async-done(((f32[256,896]{1,0:T(8,128)}, f32[256,896]{1,0:T(8,128)}, f32[256,896]{1,0:T(8,128)}), (f32[256,896]{1,0:T(8,128)}, f32[256,896]{1,0:T(8,128)}, f32[256,896]{1,0:T(8,128)})) %all-reduce.3.cloned.1.call-update) | async-done | bytes 2752528 | tf_op jit(solution)/shard_map/psum | solution.py:38
  446.3 2.2 multiply_convert_fusion
  448.6 0.0 copy-start.2
  448.6 0.3 fusion.9
  448.9 0.7 copy-done.2
  449.6 1.0 convolution_add_fusion
  450.6 0.0 reduce-scatter.5.cloned.1.call-update
  450.7 0.0 reduce-scatter.3.cloned.1.call-start
  450.7 1.0 fusion.7
  451.7 0.0 reduce-scatter.3.cloned.1.call-update
  451.7 0.3 fusion.4
  452.1 1.0 copy.10
  453.1 0.3 fusion.3
  453.4 1.0 copy.11
  454.4 1.1 fusion.2
  455.5 69.6 %reduce-scatter.5.cloned.1.call-done = f32[16,256]{1,0:T(8,128)} async-done(((f32[256,256]{1,0:T(8,128)}), f32[16,256]{1,0:T(8,128)}) %reduce-scatter.5.cloned.1.call-update) | async-done | bytes 16400 | tf_op jit(solution)/shard_map/reduce_scatter | solution.py:49
  525.1 1.3 convert_element_type.34
  526.5 84.9 %reduce-scatter.3.cloned.1.call-done = f32[16,256]{1,0:T(8,128)} async-done(((f32[256,256]{1,0:T(8,128)}), f32[16,256]{1,0:T(8,128)}) %reduce-scatter.3.cloned.1.call-update) | async-done | bytes 16400 | tf_op jit(solution)/shard_map/reduce_scatter | solution.py:43
  611.3 1.3 convert_element_type.31
Async XLA Ops:
  7.2 72.5 %copy-start = (bf16[256,896]{1,0:T(8,128)(2,1)S(1)}, bf16[256,896]{1,0:T(8,128)(2,1)}, u32[]{:S(2)}) copy-start(bf16[256,896]{1,0:T(8,128)(2,1)} %param.6) | copy-start | bytes 1376260
  7.2 39.6 %copy-start.3 = (bf16[16,256]{1,0:T(8,128)(2,1)S(1)}, bf16[16,256]{1,0:T(8,128)(2,1)}, u32[]{:S(2)}) copy-start(bf16[16,256]{1,0:T(8,128)(2,1)} %param.9) | copy-start | bytes 24580
  7.2 439.1 %all-reduce.3.cloned.1.call-start = ((), (), s32[]{:S(2)}) async-start(), calls=%async_computation.4 | async-start | bytes 5505024 | tf_op jit(solution)/shard_map/psum | solution.py:38
  79.6 1.2 copy-start.1
  82.2 443.0 %reduce-scatter.5.cloned.1.call-start = ((), (), s32[]{:S(2)}) async-start(), calls=%async_computation.3 | async-start | bytes 278528 | tf_op jit(solution)/shard_map/reduce_scatter | solution.py:49
  448.6 1.0 copy-start.2
  450.7 160.7 %reduce-scatter.3.cloned.1.call-start = ((), (), s32[]{:S(2)}) async-start(), calls=%async_computation.2 | async-start | bytes 278528 | tf_op jit(solution)/shard_map/reduce_scatter | solution.py:43
Sparse Core Ops, SparseCore 0:
  82.3 364.0 all-reduce.2
  450.8 74.3 reduce-scatter.4
  528.2 83.1 reduce-scatter.2
where the time goes:
time: 631 us; the launch traced here: 619 us
  waiting for transfers between devices  519 us (82%)
  blocking collectives  70.1 us (11%)
  between operations  13.8 us (2%)
  matrix products  8.89 us (1%)
    psum x1, waiting for transfers between devices, on_device(): gate_sum, up_sum = lax.psum((gate_part, up_part), 'dp')  364 us
    reduce_scatter x1, waiting for transfers between devices, on_device(): lax.psum_scatter(jnp.dot(hidden, down_weight, preferred_element_type=jnp....  84.9 us
    reduce_scatter x1, waiting for transfers between devices, on_device(): lax.psum_scatter(contract_last(grad_gate, gate_weight) + contract_last(gr...  69.6 us
    all_gather x1, blocking collectives, on_device(): gathered = lax.all_gather(tokens, 'mp', axis=0, tiled=True)  39.5 us
    all_gather x1, blocking collectives, on_device(): grad_output = lax.all_gather(cotangent, 'mp', axis=0, tiled=True)  30.6 us
  transfers between devices with their start and end apart: 3, of which 3 were waited for; matrix products, arithmetic and copies ran while one was open for 1% of the time, Pallas kernels for 0%

commit v1 on v0

v1 whole, which is shorter than its diff:
```python
import math

import jax
import jax.numpy as jnp
from jax import lax
from jax.experimental import pallas as pl
from jax.experimental.pallas import tpu as pltpu
from jax.sharding import PartitionSpec as P

MESH = pl.DeviceIdType.MESH
F32 = jnp.float32
BF16 = jnp.bfloat16
RING = 8
ROWS = 16
CODE_SCALE = float(2**18)


def encode(x):
    x = x * CODE_SCALE
    return (x * x * (x * jnp.abs(x))).astype(BF16)


def decode(code):
    y = code.astype(F32)
    root = lax.rsqrt(lax.rsqrt(jnp.abs(y))) * (1.0 / CODE_SCALE)
    return jnp.where(y < 0, -root, root)


def dot(left, right):
    return jnp.dot(left, right, preferred_element_type=F32)


def dot_last(left, right):
    return lax.dot_general(left, right, (((1,), (1,)), ((), ())), preferred_element_type=F32)


def dot_first(left, right):
    return lax.dot_general(left, right, (((0,), (0,)), ((), ())), preferred_element_type=F32)


def kernel(
    tok_ref, cot_ref, wg_hbm, wu_hbm, wd_hbm,
    out_ref, tgrad_ref, ggrad_ref, ugrad_ref, dgrad_ref,
    wg, wu, wd, sg, su, sd,
    tg, cg, ts, cs, acc,
    sendp, recvp, sendm, recvm, sendz, recvz,
    hgu, part, parts,
    load_sem, wsib_ss, wsib_rs, gat_ss, gat_rs, fwd_ss, fwd_rs,
    rp_ss, rp_rs, rm_ss, rm_rs, z_ss, z_rs,
    ap_ss, ap_rs, am_ss, am_rs, af_ss, af_rs, o_ss, o_rs,
):
    dp, mp = lax.axis_index("dp"), lax.axis_index("mp")
    core, y, zh = dp % 2, (dp // 2) % RING, dp // 16
    sib = (dp + 1 - 2 * core, mp)
    yplus = (zh * 16 + ((y + 1) % RING) * 2 + core, mp)
    yminus = (zh * 16 + ((y + RING - 1) % RING) * 2 + core, mp)
    zother = ((1 - zh) * 16 + y * 2 + core, mp)
    n_mp = 16
    factor = 1.0 / math.sqrt(ROWS * n_mp)

    def remote(src, dst, ss, rs, to):
        return pltpu.make_async_remote_copy(
            src_ref=src, dst_ref=dst, send_sem=ss, recv_sem=rs,
            device_id=to, device_id_type=MESH,
        )

    def rows16(index):
        return pl.ds(pl.multiple_of(index * ROWS, ROWS), ROWS)

    loads = [
        pltpu.make_async_copy(src, dst, load_sem.at[i])
        for i, (src, dst) in enumerate(((wg_hbm, wg), (wu_hbm, wu), (wd_hbm, wd)))
    ]
    for copy in loads:
        copy.start()

    barrier = pltpu.get_barrier_semaphore()
    for to in (sib, yplus, yminus, zother):
        pl.semaphore_signal(barrier, inc=1, device_id=to, device_id_type=MESH)
    for k in range(1, n_mp):
        pl.semaphore_signal(barrier, inc=1, device_id=(dp, (mp + k) % n_mp), device_id_type=MESH)
    pl.semaphore_wait(barrier, 4 + n_mp - 1)

    gathers = []
    for i, (src, dst) in enumerate(((tok_ref, tg), (cot_ref, cg))):
        group = []
        for k in range(1, n_mp):
            copy = remote(
                src, dst.at[rows16(mp)], gat_ss.at[i, k], gat_rs.at[i, k], (dp, (mp + k) % n_mp)
            )
            copy.start()
            group.append(copy)
        gathers.append(group)
    wsib = [
        remote(src, dst, wsib_ss.at[i], wsib_rs.at[i], sib)
        for i, (src, dst) in enumerate(((wg_hbm, sg), (wu_hbm, su), (wd_hbm, sd)))
    ]
    for copy in wsib:
        copy.start()
    tg[rows16(mp), :] = tok_ref[...]
    cg[rows16(mp), :] = cot_ref[...]

    mine = pl.ds(pl.multiple_of(core * 128, 128), 128)
    theirs = pl.ds(pl.multiple_of((1 - core) * 128, 128), 128)

    def block(array, index):
        return acc[array, rows16(index), :]

    ring_p = [[None] * 3 for _ in range(4)]
    ring_m = [[None] * 3 for _ in range(3)]

    def send_p(step, array, value):
        sendp[step, array] = encode(value)
        ring_p[step][array] = remote(
            sendp.at[step, array], recvp.at[step, array],
            rp_ss.at[step, array], rp_rs.at[step, array], yplus,
        )
        ring_p[step][array].start()

    def send_m(step, array, value):
        sendm[step, array] = encode(value)
        ring_m[step][array] = remote(
            sendm.at[step, array], recvm.at[step, array],
            rm_ss.at[step, array], rm_rs.at[step, array], yminus,
        )
        ring_m[step][array].start()

    def first_hop(array):
        send_p(0, array, block(array, (y + 4) % RING))
        send_m(0, array, block(array, (y + 5) % RING))

    forwards = []
    for i, (full, half) in enumerate(((tg, ts), (cg, cs))):
        for copy in gathers[i]:
            copy.wait_recv()
        forward = remote(full.at[theirs], half, fwd_ss.at[i], fwd_rs.at[i], sib)
        forward.start()
        forwards.append(forward)
        if i == 0:
            loads[0].wait()
            loads[1].wait()
            wsib[0].wait_recv()
            wsib[1].wait_recv()
            forward.wait_recv()
            acc[0] = dot(tg[mine, :], wg[...]) + dot(ts[...], sg[...])
            first_hop(0)
            acc[1] = dot(tg[mine, :], wu[...]) + dot(ts[...], su[...])
            first_hop(1)
        else:
            loads[2].wait()
            wsib[2].wait_recv()
            forward.wait_recv()
            acc[2] = dot_last(cg[mine, :], wd[...]) + dot_last(cs[...], sd[...])
            first_hop(2)

    for step in range(3):
        for array in range(3):
            ring_p[step][array].wait_recv()
            send_p(
                step + 1, array,
                block(array, (y + 3 - step) % RING) + decode(recvp[step, array]),
            )
            ring_m[step][array].wait_recv()
            if step < 2:
                send_m(
                    step + 1, array,
                    block(array, (y + 6 + step) % RING) + decode(recvm[step, array]),
                )
            else:
                acc[array, rows16(y), :] += decode(recvm[2, array])
    swaps = []
    for array in range(3):
        ring_p[3][array].wait_recv()
        value = block(array, y) + decode(recvp[3, array])
        acc[array, rows16(y), :] = value
        sendz[array] = encode(value)
        swap = remote(sendz.at[array], recvz.at[array], z_ss.at[array], z_rs.at[array], zother)
        swap.start()
        swaps.append(swap)
    for swap in swaps:
        swap.wait_recv()
    gate = block(0, y) + decode(recvz[0])
    up = block(1, y) + decode(recvz[1])
    grad_hidden = block(2, y) + decode(recvz[2])
    sig = jax.nn.sigmoid(gate)
    own = core * RING + y
    hgu[own, 0] = (gate * sig * up).astype(BF16)
    hgu[own, 1] = (grad_hidden * up * sig * (1.0 + gate * (1.0 - sig))).astype(BF16)
    hgu[own, 2] = (grad_hidden * gate * sig).astype(BF16)

    started = []

    def pass_on(index, ss, rs, to):
        copy = remote(hgu.at[index], hgu.at[index], ss, rs, to)
        copy.start()
        started.append(copy)
        return copy

    to_sib = []
    copy_p = pass_on(own, ap_ss.at[0], ap_rs.at[0], yplus)
    copy_m = pass_on(own, am_ss.at[0], am_rs.at[0], yminus)
    to_sib.append(pass_on(own, af_ss.at[0], af_rs.at[0], sib))
    for step in range(4):
        index = core * RING + (y + 7 - step) % RING
        copy_p.wait_recv()
        if step < 3:
            copy_p = pass_on(index, ap_ss.at[step + 1], ap_rs.at[step + 1], yplus)
        to_sib.append(pass_on(index, af_ss.at[1 + step], af_rs.at[1 + step], sib))
        if step < 3:
            index = core * RING + (y + 1 + step) % RING
            copy_m.wait_recv()
            if step < 2:
                copy_m = pass_on(index, am_ss.at[step + 1], am_rs.at[step + 1], yminus)
            to_sib.append(pass_on(index, af_ss.at[5 + step], af_rs.at[5 + step], sib))
    for copy in to_sib:
        copy.wait_recv()

    hidden = hgu[:, 0].reshape(256, -1)
    grad_gate = hgu[:, 1].reshape(256, -1)
    grad_up = hgu[:, 2].reshape(256, -1)
    total_out = dot(hidden, wd[...])
    total_tg = dot_last(grad_gate, wg[...]) + dot_last(grad_up, wu[...])
    part[:, 0] = total_out.astype(BF16).reshape(n_mp, ROWS, 256)
    part[:, 1] = total_tg.astype(BF16).reshape(n_mp, ROWS, 256)
    finals = []
    for k in range(1, n_mp):
        to = (mp + k) % n_mp
        copy = remote(part.at[to], parts.at[k], o_ss.at[k], o_rs.at[k], (dp, to))
        copy.start()
        finals.append(copy)

    ggrad_ref[...] = (dot_first(tg[...], grad_gate) * factor).astype(BF16)
    ugrad_ref[...] = (dot_first(tg[...], grad_up) * factor).astype(BF16)
    dgrad_ref[...] = (dot_first(hidden, cg[...]) * factor).astype(BF16)

    sum_out = part[mp, 0].astype(F32)
    sum_tg = part[mp, 1].astype(F32)
    for k in range(1, n_mp):
        finals[k - 1].wait_recv()
        sum_out += parts[k, 0].astype(F32)
        sum_tg += parts[k, 1].astype(F32)
    out_ref[...] = sum_out.astype(BF16)
    tgrad_ref[...] = sum_tg.astype(BF16)

    for copy in gathers[0] + gathers[1] + wsib + forwards + swaps + started + finals:
        copy.wait_send()
    for hops in ring_p + ring_m:
        for copy in hops:
            copy.wait_send()


def on_device(tokens, gate_weight, up_weight, down_weight, cotangent):
    rows, width = tokens.shape
    units = gate_weight.shape[1]
    vmem = pl.BlockSpec(memory_space=pltpu.VMEM)
    hbm = pl.BlockSpec(memory_space=pl.ANY)
    dma = pltpu.SemaphoreType.DMA
    wide = pltpu.VMEM((width, units), BF16)
    tall = pltpu.VMEM((units, width), BF16)
    return pl.pallas_call(
        kernel,
        out_shape=(
            jax.ShapeDtypeStruct((rows, width), BF16),
            jax.ShapeDtypeStruct((rows, width), BF16),
            jax.ShapeDtypeStruct((width, units), BF16),
            jax.ShapeDtypeStruct((width, units), BF16),
            jax.ShapeDtypeStruct((units, width), BF16),
        ),
        in_specs=[vmem, vmem, hbm, hbm, hbm],
        out_specs=[vmem] * 5,
        scratch_shapes=[
            wide, wide, tall, wide, wide, tall,
            pltpu.VMEM((256, width), BF16), pltpu.VMEM((256, width), BF16),
            pltpu.VMEM((128, width), BF16), pltpu.VMEM((128, width), BF16),
            pltpu.VMEM((3, 128, units), F32),
            pltpu.VMEM((4, 3, ROWS, units), BF16), pltpu.VMEM((4, 3, ROWS, units), BF16),
            pltpu.VMEM((3, 3, ROWS, units), BF16), pltpu.VMEM((3, 3, ROWS, units), BF16),
            pltpu.VMEM((3, ROWS, units), BF16), pltpu.VMEM((3, ROWS, units), BF16),
            pltpu.VMEM((16, 3, ROWS, units), BF16),
            pltpu.VMEM((16, 2, ROWS, width), BF16), pltpu.VMEM((16, 2, ROWS, width), BF16),
            dma((3,)), dma((3,)), dma((3,)), dma((2, 16)), dma((2, 16)), dma((2,)), dma((2,)),
            dma((4, 3)), dma((4, 3)), dma((3, 3)), dma((3, 3)), dma((3,)), dma((3,)),
            dma((4,)), dma((4,)), dma((3,)), dma((3,)), dma((8,)), dma((8,)),
            dma((16,)), dma((16,)),
        ],
        compiler_params=pltpu.CompilerParams(
            collective_id=0, has_side_effects=True, vmem_limit_bytes=40 * 2**20
        ),
    )(tokens, cotangent, gate_weight, up_weight, down_weight)


def solution(mesh):
    in_specs = (P("mp", "dp"), P("dp", "mp"), P("dp", "mp"), P("mp", "dp"), P("mp", "dp"))
    out_specs = (P("mp", "dp"), P("mp", "dp"), P("dp", "mp"), P("dp", "mp"), P("mp", "dp"))
    return jax.shard_map(
        on_device, mesh=mesh, in_specs=in_specs, out_specs=out_specs, check_vma=False
    )
```

time: 631 us -> 75.8 us (0.12); the launches traced: 619 us -> 75.4 us
  waiting for transfers between devices: 519 us -> 0 us
  blocking collectives: 70.1 us -> 0 us
  Pallas kernels: 0 us -> 66.8 us
  between operations: 13.8 us -> 0.66 us
  matrix products: 8.89 us -> 0 us
    psum x1 -> x0, waiting for transfers between devices: 364 us -> none  [on_device(): gate_sum, up_sum = lax.psum((gate_part, up_part), 'dp')]
    reduce_scatter x2 -> x0, waiting for transfers between devices: 155 us -> none  [the longest x1 84.9 us: on_device(): lax.psum_scatter(jnp.dot(hidden, down_weight, preferred_element_type=jnp....]
    all_gather x2 -> x0, blocking collectives: 70.1 us -> none  [the longest x1 39.5 us: on_device(): gathered = lax.all_gather(tokens, 'mp', axis=0, tiled=True)]
    pallas_call x0 -> x1, Pallas kernels: none -> 66.8 us  [on_device(): pl.pallas_call(kernel, out_shape=(jax.ShapeDtypeStruct((rows, width), BF1...]
    dot_general x9 -> x0, matrix products: 8.89 us -> none  [the longest x3 2.64 us: contract_last(): lax.dot_general(left_side, right_side, (((1,), (1,)), ((), ())), preferre...]
  transfers between devices with their start and end apart: 3 -> 0, of which waited for: 3 -> 0; matrix products, arithmetic and copies ran while one was open for 1% -> 0% of each run, Pallas kernels for 0% -> 0%
where the time goes in v1:
time: 75.8 us; the launch traced here: 75.4 us
  Pallas kernels  66.8 us (88%)
  local copies, waits for them, and re-layouts  7.94 us (10%)
    pallas_call x1, Pallas kernels, on_device(): pl.pallas_call(kernel, out_shape=(jax.ShapeDtypeStruct((rows, width), BF1...  66.8 us
    unnamed x15, local copies, waits for them, and re-layouts  7.94 us

profile of v1, /device:TPU:1, one launch (start us, length us, event | category | flops | bytes accessed | tf_op | source)
XLA Modules:
  0.0 75.4 jit_solution(8837046277467959975)
XLA Ops:
  0.6 0.0 copy-start
  0.6 1.0 %copy-done = bf16[256,896]{1,0:T(8,128)(2,1)S(1)} copy-done((bf16[256,896]{1,0:T(8,128)(2,1)S(1)}, bf16[256,896]{1,0:T(8,128)(2,1)}, u32[]{:S(2)}) %copy-start) | copy-done | bytes 458776
  1.7 0.0 copy-start.1
  1.7 1.0 %copy-done.1 = bf16[256,896]{1,0:T(8,128)(2,1)S(1)} copy-done((bf16[256,896]{1,0:T(8,128)(2,1)S(1)}, bf16[256,896]{1,0:T(8,128)(2,1)}, u32[]{:S(2)}) %copy-start.1) | copy-done | bytes 458776
  2.7 0.0 copy-start.2
  2.7 1.0 %copy-done.2 = bf16[896,256]{1,0:T(8,128)(2,1)S(1)} copy-done((bf16[896,256]{1,0:T(8,128)(2,1)S(1)}, bf16[896,256]{1,0:T(8,128)(2,1)}, u32[]{:S(2)}) %copy-start.2) | copy-done | bytes 458776
  3.7 0.0 copy-start.3
  3.7 0.7 copy-done.3
  4.4 0.0 copy-start.4
  4.4 0.7 copy-done.4
  5.1 66.8 %shard_map.92 = (bf16[16,256]{1,0:T(8,128)(2,1)S(1)}, bf16[16,256]{1,0:T(8,128)(2,1)S(1)}, bf16[256,896]{1,0:T(8,128)(2,1)S(1)}, bf16[256,896]{1,0:T(8,128)(2,1)S(1)}, bf16[896,256]{1,0:T(8,128)(2,1)S(1)}) custom-call(bf16[16,256]{1,0:T(8,128)(2,1)S(1)} %copy-done.3, bf16[16,256]{1,0:T(8,128)(2,1)S(1)} %copy-done.4, bf16[256,896]{1,0:T(8,128)(2,1)S(1)} %copy-done, ...), custom_call_target="tpu_custom_call" | custom-call | tf_op jit(solution)/shard_map/pallas_call | solution.py:260
  71.9 0.6 copy.15
  72.5 0.6 copy.16
  73.1 0.8 %copy.17 = bf16[256,896]{1,0:T(8,128)(2,1)} copy(bf16[256,896]{1,0:T(8,128)(2,1)S(1)} %get-tuple-element.12) | data formatting | bytes 917504
  73.9 0.8 %copy.18 = bf16[256,896]{1,0:T(8,128)(2,1)} copy(bf16[256,896]{1,0:T(8,128)(2,1)S(1)} %get-tuple-element.13) | data formatting | bytes 917504
  74.7 0.8 %copy.19 = bf16[896,256]{1,0:T(8,128)(2,1)} copy(bf16[896,256]{1,0:T(8,128)(2,1)S(1)} %get-tuple-element.14) | data formatting | bytes 917504
Async XLA Ops:
  0.6 1.0 %copy-start = (bf16[256,896]{1,0:T(8,128)(2,1)S(1)}, bf16[256,896]{1,0:T(8,128)(2,1)}, u32[]{:S(2)}) copy-start(bf16[256,896]{1,0:T(8,128)(2,1)} %wg_hbm.1) | copy-start | bytes 1376260
  1.7 1.0 %copy-start.1 = (bf16[256,896]{1,0:T(8,128)(2,1)S(1)}, bf16[256,896]{1,0:T(8,128)(2,1)}, u32[]{:S(2)}) copy-start(bf16[256,896]{1,0:T(8,128)(2,1)} %wu_hbm.1) | copy-start | bytes 1376260
  2.7 1.0 %copy-start.2 = (bf16[896,256]{1,0:T(8,128)(2,1)S(1)}, bf16[896,256]{1,0:T(8,128)(2,1)}, u32[]{:S(2)}) copy-start(bf16[896,256]{1,0:T(8,128)(2,1)} %wd_hbm.1) | copy-start | bytes 1376260
  3.7 0.7 copy-start.3
  4.4 0.7 copy-start.4

commit v2 on v0

v2 whole, which is shorter than its diff:
```python
import math

import jax
import jax.numpy as jnp
from jax import lax
from jax.experimental import pallas as pl
from jax.experimental.pallas import tpu as pltpu
from jax.sharding import PartitionSpec as P

MESH = pl.DeviceIdType.MESH
F32 = jnp.float32
BF16 = jnp.bfloat16
RING = 8
ROWS = 16
HALF = RING * ROWS
N_MP = 16
VMEM_LIMIT = 62 * 2**20
CODE_SCALE = float(2**18)


def encode(x):
    x = x * CODE_SCALE
    return (x * x * (x * jnp.abs(x))).astype(BF16)


def decode(code):
    y = code.astype(F32)
    root = lax.rsqrt(lax.rsqrt(jnp.abs(y))) * (1.0 / CODE_SCALE)
    return jnp.where(y < 0, -root, root)


def dot(left, right):
    return jnp.dot(left, right, preferred_element_type=F32)


def dot_last(left, right):
    return lax.dot_general(left, right, (((1,), (1,)), ((), ())), preferred_element_type=F32)


def dot_first(left, right):
    return lax.dot_general(left, right, (((0,), (0,)), ((), ())), preferred_element_type=F32)


def kernel(
    tok_hbm, cot_hbm, wg_hbm, wu_hbm, wd_hbm,
    out_hbm, tgrad_hbm, ggrad_hbm, ugrad_hbm, dgrad_hbm,
    wg, wu, wd, sg, su, sd,
    mine, rows, other, full, acc, send, recv, sendz, recvz,
    hid, gug, part, parts, small, ggrad, ugrad, dgrad,
    load_sem, mine_sem, wsib_ss, wsib_rs, gat_ss, gat_rs, oth_ss, oth_rs,
    rs_ss, rs_rs, z_ss, z_rs, ag_ss, ag_rs, half_ss, half_rs, o_ss, o_rs, res_sem,
):
    dp, mp = lax.axis_index("dp"), lax.axis_index("mp")
    core, y, zh = dp % 2, (dp // 2) % RING, dp // 16
    rot = mp % RING
    row_core = mp // RING
    sib = (dp + 1 - 2 * core, mp)
    zother = ((1 - zh) * 16 + y * 2 + core, mp)
    factor = 1.0 / math.sqrt(ROWS * N_MP)

    def remote(src, dst, ss, rs, to):
        return pltpu.make_async_remote_copy(
            src_ref=src, dst_ref=dst, send_sem=ss, recv_sem=rs,
            device_id=to, device_id_type=MESH,
        )

    def await_copy(ref, sem):
        pltpu.make_async_copy(ref, ref, sem).wait()

    def along_y(hops):
        return (zh * 16 + ((y + hops + RING) % RING) * 2 + core, mp)

    def local_block(ring_index):
        return (ring_index + 2 * RING + rot) % RING

    def rows16(index):
        return pl.ds(pl.multiple_of(index * ROWS, ROWS), ROWS)

    started = []

    def start(copy):
        copy.start()
        started.append(copy)
        return copy

    own_loads = [
        pltpu.make_async_copy(src, mine.at[i], mine_sem.at[i])
        for i, src in enumerate((tok_hbm, cot_hbm))
    ]
    for copy in own_loads:
        copy.start()
    loads = [
        pltpu.make_async_copy(src, dst, load_sem.at[i])
        for i, (src, dst) in enumerate(((wg_hbm, wg), (wu_hbm, wu), (wd_hbm, wd)))
    ]
    for copy in loads:
        copy.start()

    peers = [sib, zother] + [along_y(hops) for hops in range(1, RING)]
    for k in range(1, N_MP):
        peers += [(dp, (mp + k) % N_MP), (sib[0], (mp + k) % N_MP)]
    barrier = pltpu.get_barrier_semaphore()
    for to in peers:
        pl.semaphore_signal(barrier, inc=1, device_id=to, device_id_type=MESH)
    pl.semaphore_wait(barrier, len(peers))

    worker = dp - core + row_core
    at_home = row_core == core
    gathers = []
    for i in range(2):
        own_loads[i].wait()
        target = rows.at[core, i, rows16(rot)]
        for k in range(1, N_MP):
            start(
                remote(
                    mine.at[i], target, gat_ss.at[i, k], gat_rs.at[i, core, rot],
                    (worker, (mp + k) % N_MP),
                )
            )
        stay = pltpu.make_async_copy(mine.at[i], target, gat_rs.at[i, core, rot])
        cross = remote(mine.at[i], target, gat_ss.at[i, 0], gat_rs.at[i, core, rot], sib)
        pl.when(at_home)(stay.start)
        pl.when(jnp.logical_not(at_home))(cross.start)
        gathers.append(cross)
        weights = ((wg_hbm, sg, 0), (wu_hbm, su, 1)) if i == 0 else ((wd_hbm, sd, 2),)
        for src, dst, j in weights:
            start(remote(src, dst, wsib_ss.at[j], wsib_rs.at[j], sib))

    def send_sums(array):
        for n, hops in enumerate((4, 3, -3, 2, -2, 1, -1)):
            index = local_block(y + hops)
            send[array, n] = encode(acc[array, rows16(index), :])
            start(
                remote(
                    send.at[array, n], recv.at[array, n],
                    rs_ss.at[array, n], rs_rs.at[array, n], along_y(hops),
                )
            )

    for i in range(2):
        for side in range(2):
            for b in range(RING):
                await_copy(rows.at[side, i, pl.ds(b * ROWS, ROWS)], gat_rs.at[i, side, b])
        near, far = rows[core, i], rows[1 - core, i]
        if i == 0:
            loads[0].wait()
            await_copy(sg, wsib_rs.at[0])
            acc[0] = dot(near, wg[...]) + dot(far, sg[...])
            send_sums(0)
            loads[1].wait()
            await_copy(su, wsib_rs.at[1])
            acc[1] = dot(near, wu[...]) + dot(far, su[...])
            send_sums(1)
        else:
            loads[2].wait()
            await_copy(sd, wsib_rs.at[2])
            acc[2] = dot_last(near, wd[...]) + dot_last(far, sd[...])
            send_sums(2)

    start(remote(rows.at[1 - core], other, oth_ss, oth_rs, sib))

    def collect(array):
        total = acc[array, rows16(local_block(y)), :]
        for n in range(RING - 1):
            await_copy(recv.at[array, n], rs_rs.at[array, n])
            total += decode(recv[array, n])
        sendz[array] = encode(total)
        start(remote(sendz.at[array], recvz.at[array], z_ss.at[array], z_rs.at[array], zother))
        return total

    gate, up, grad_hidden = collect(0), collect(1), collect(2)
    own = core * RING + local_block(y)
    hops_order = (1, -1, 2, -2, 3, -3, 4)

    def block_of(hops):
        return core * RING + local_block(y - hops)

    def spread(ref, which):
        for n, hops in enumerate(hops_order):
            start(
                remote(
                    ref.at[own], ref.at[own], ag_ss.at[which, n], ag_rs.at[which, n],
                    along_y(hops),
                )
            )

    await_copy(recvz.at[0], z_rs.at[0])
    await_copy(recvz.at[1], z_rs.at[1])
    gate += decode(recvz[0])
    up += decode(recvz[1])
    sig = jax.nn.sigmoid(gate)
    hid[own] = (gate * sig * up).astype(BF16)
    spread(hid, 0)
    await_copy(recvz.at[2], z_rs.at[2])
    grad_hidden += decode(recvz[2])
    gug[own, 0] = (grad_hidden * up * sig * (1.0 + gate * (1.0 - sig))).astype(BF16)
    gug[own, 1] = (grad_hidden * gate * sig).astype(BF16)
    spread(gug, 1)

    batches = ((0, 1, -1, 2, -2), (3, -3, 4))
    finals = []

    def arrive(ref, which, batch):
        for hops in batch:
            if hops:
                n = hops_order.index(hops)
                await_copy(ref.at[block_of(hops)], ag_rs.at[which, n])

    def deliver(which, side, batch, values):
        for n, hops in enumerate(batch):
            slot = (hops + RING) % RING * 2 + side
            index = block_of(hops)
            src, dst = part.at[which, slot], parts.at[which, mp]
            part[which, slot] = values[n * ROWS : (n + 1) * ROWS]
            to = (sib[0] if side else dp, index)
            copy = remote(src, dst, o_ss.at[which, slot], o_rs.at[which, mp], to)
            if side == 0:
                stay = pltpu.make_async_copy(src, dst, o_rs.at[which, mp])
                pl.when(index == mp)(stay.start)
                pl.when(index != mp)(copy.start)
                finals.append((copy, index))
            else:
                start(copy)

    def rows_of(ref, batch):
        return jnp.concatenate([ref[block_of(hops)] for hops in batch], axis=0)

    def my_half(ref):
        return ref.at[pl.ds(pl.multiple_of(core * RING, RING), RING)]

    def their_half(ref):
        return ref.at[pl.ds(pl.multiple_of((1 - core) * RING, RING), RING)]

    for batch in batches:
        arrive(hid, 0, batch)
        hidden = rows_of(hid, batch)
        for side, down_w in enumerate((wd, sd)):
            deliver(0, side, batch, dot(hidden, down_w[...]).astype(BF16))
    start(remote(my_half(hid), my_half(hid), half_ss.at[0], half_rs.at[0], sib))

    results = []

    def store(src, dst):
        copy = pltpu.make_async_copy(src, dst, res_sem.at[len(results)])
        copy.start()
        results.append(copy)

    await_copy(other, oth_rs)
    for i in range(2):
        full[i, pl.ds(pl.multiple_of(core * HALF, HALF), HALF), :] = rows[core, i]
        full[i, pl.ds(pl.multiple_of((1 - core) * HALF, HALF), HALF), :] = other[i]

    def grads_tokens(batch):
        arrive(gug, 1, batch)
        grad_gate = jnp.concatenate([gug[block_of(hops), 0] for hops in batch], axis=0)
        grad_up = jnp.concatenate([gug[block_of(hops), 1] for hops in batch], axis=0)
        for side, (gate_w, up_w) in enumerate(((wg, wu), (sg, su))):
            value = dot_last(grad_gate, gate_w[...]) + dot_last(grad_up, up_w[...])
            deliver(1, side, batch, value.astype(BF16))

    grads_tokens(batches[0])
    await_copy(their_half(hid), half_rs.at[0])
    dgrad[...] = (dot_first(hid[...].reshape(2 * HALF, -1), full[1]) * factor).astype(BF16)
    store(dgrad, dgrad_hbm)
    grads_tokens(batches[1])

    start(remote(my_half(gug), my_half(gug), half_ss.at[1], half_rs.at[1], sib))
    await_copy(their_half(gug), half_rs.at[1])
    grad_gate = gug[:, 0].reshape(2 * HALF, -1)
    grad_up = gug[:, 1].reshape(2 * HALF, -1)
    ggrad[...] = (dot_first(full[0], grad_gate) * factor).astype(BF16)
    store(ggrad, ggrad_hbm)
    ugrad[...] = (dot_first(full[0], grad_up) * factor).astype(BF16)
    store(ugrad, ugrad_hbm)

    for which, target in enumerate((out_hbm, tgrad_hbm)):
        total = jnp.zeros((ROWS, 256), F32)
        for k in range(N_MP):
            await_copy(parts.at[which, k], o_rs.at[which, k])
            total += parts[which, k].astype(F32)
        small[which] = total.astype(BF16)
        store(small.at[which], target)

    for copy in started:
        copy.wait_send()
    for i in range(2):
        pl.when(jnp.logical_not(at_home))(gathers[i].wait_send)
    for copy, index in finals:
        pl.when(index != mp)(copy.wait_send)
    for copy in results:
        copy.wait()


def copy_out(*refs):
    sources, targets, staged, sems = refs[:5], refs[5:10], refs[10:15], refs[15]
    loads = [
        pltpu.make_async_copy(src, mid, sems.at[0, i])
        for i, (src, mid) in enumerate(zip(sources, staged))
    ]
    stores = [
        pltpu.make_async_copy(mid, dst, sems.at[1, i])
        for i, (mid, dst) in enumerate(zip(staged, targets))
    ]
    for copy in loads:
        copy.start()
    for load, store in zip(loads, stores):
        load.wait()
        store.start()
    for copy in stores:
        copy.wait()


def on_device(tokens, gate_weight, up_weight, down_weight, cotangent):
    count, width = tokens.shape
    units = gate_weight.shape[1]
    hbm = pl.BlockSpec(memory_space=pltpu.HBM)
    dma = pltpu.SemaphoreType.DMA

    def vmem(*shape, dtype=BF16):
        return pltpu.VMEM(shape, dtype)

    shapes = (
        jax.ShapeDtypeStruct((count, width), BF16),
        jax.ShapeDtypeStruct((count, width), BF16),
        jax.ShapeDtypeStruct((width, units), BF16),
        jax.ShapeDtypeStruct((width, units), BF16),
        jax.ShapeDtypeStruct((units, width), BF16),
    )
    results = pl.pallas_call(
        kernel,
        out_shape=shapes,
        in_specs=[hbm] * 5,
        out_specs=[hbm] * 5,
        scratch_shapes=[
            vmem(width, units), vmem(width, units), vmem(units, width),
            vmem(width, units), vmem(width, units), vmem(units, width),
            vmem(2, ROWS, width), vmem(2, 2, HALF, width), vmem(2, HALF, width),
            vmem(2, 2 * HALF, width), vmem(3, HALF, units, dtype=F32),
            vmem(3, RING - 1, ROWS, units), vmem(3, RING - 1, ROWS, units),
            vmem(3, ROWS, units), vmem(3, ROWS, units),
            vmem(N_MP, ROWS, units), vmem(N_MP, 2, ROWS, units),
            vmem(2, N_MP, ROWS, width), vmem(2, N_MP, ROWS, width), vmem(2, ROWS, width),
            vmem(width, units), vmem(width, units), vmem(units, width),
            dma((3,)), dma((2,)), dma((3,)), dma((3,)), dma((2, N_MP)), dma((2, 2, RING)),
            dma(()), dma(()),
            dma((3, RING - 1)), dma((3, RING - 1)), dma((3,)), dma((3,)),
            dma((2, RING - 1)), dma((2, RING - 1)), dma((2,)), dma((2,)),
            dma((2, N_MP)), dma((2, N_MP)), dma((5,)),
        ],
        compiler_params=pltpu.CompilerParams(
            collective_id=0, has_side_effects=True, vmem_limit_bytes=VMEM_LIMIT
        ),
    )(tokens, cotangent, gate_weight, up_weight, down_weight)
    return pl.pallas_call(
        copy_out,
        out_shape=shapes,
        in_specs=[hbm] * 5,
        out_specs=[hbm] * 5,
        scratch_shapes=[pltpu.VMEM(s.shape, s.dtype) for s in shapes] + [dma((2, 5))],
        compiler_params=pltpu.CompilerParams(vmem_limit_bytes=VMEM_LIMIT),
    )(*results)


def solution(mesh):
    in_specs = (P("mp", "dp"), P("dp", "mp"), P("dp", "mp"), P("mp", "dp"), P("mp", "dp"))
    out_specs = (P("mp", "dp"), P("mp", "dp"), P("dp", "mp"), P("dp", "mp"), P("mp", "dp"))
    return jax.shard_map(
        on_device, mesh=mesh, in_specs=in_specs, out_specs=out_specs, check_vma=False
    )
```

time: 631 us -> 67.6 us (0.11); the launches traced: 619 us -> 67.4 us
  waiting for transfers between devices: 519 us -> 0 us
  blocking collectives: 70.1 us -> 0 us
  Pallas kernels: 0 us -> 66.7 us
  between operations: 13.8 us -> 0.64 us
  matrix products: 8.89 us -> 0 us
    psum x1 -> x0, waiting for transfers between devices: 364 us -> none  [on_device(): gate_sum, up_sum = lax.psum((gate_part, up_part), 'dp')]
    reduce_scatter x2 -> x0, waiting for transfers between devices: 155 us -> none  [the longest x1 84.9 us: on_device(): lax.psum_scatter(jnp.dot(hidden, down_weight, preferred_element_type=jnp....]
    all_gather x2 -> x0, blocking collectives: 70.1 us -> none  [the longest x1 39.5 us: on_device(): gathered = lax.all_gather(tokens, 'mp', axis=0, tiled=True)]
    pallas_call x0 -> x2, Pallas kernels: none -> 66.7 us  [the longest x1 64.5 us: on_device(): pl.pallas_call(kernel, out_shape=shapes, in_specs=[hbm] * 5, out_specs=[h...]
    dot_general x9 -> x0, matrix products: 8.89 us -> none  [the longest x3 2.64 us: contract_last(): lax.dot_general(left_side, right_side, (((1,), (1,)), ((), ())), preferre...]
  transfers between devices with their start and end apart: 3 -> 0, of which waited for: 3 -> 0; matrix products, arithmetic and copies ran while one was open for 1% -> 0% of each run, Pallas kernels for 0% -> 0%
where the time goes in v2:
time: 67.6 us; the launch traced here: 67.4 us
  Pallas kernels  66.7 us (99%)
    pallas_call x1, Pallas kernels, on_device(): pl.pallas_call(kernel, out_shape=shapes, in_specs=[hbm] * 5, out_specs=[h...  64.5 us
    pallas_call x1, Pallas kernels, on_device(): pl.pallas_call(copy_out, out_shape=shapes, in_specs=[hbm] * 5, out_specs=...  2.21 us

profile of v2, /device:TPU:1, one launch (start us, length us, event | category | flops | bytes accessed | tf_op | source)
XLA Modules:
  0.0 67.4 jit_solution(8265121650939056354)
XLA Ops:
  0.6 64.5 %shard_map.92 = (bf16[16,256]{1,0:T(8,128)(2,1)}, bf16[16,256]{1,0:T(8,128)(2,1)}, bf16[256,896]{1,0:T(8,128)(2,1)}, bf16[256,896]{1,0:T(8,128)(2,1)}, bf16[896,256]{1,0:T(8,128)(2,1)}) custom-call(bf16[16,256]{1,0:T(8,128)(2,1)} %tok_hbm.1, bf16[16,256]{1,0:T(8,128)(2,1)} %cot_hbm.1, bf16[256,896]{1,0:T(8,128)(2,1)} %wg_hbm.1, bf16[256,896]{1,0:T(8,128)(2,1)} %wu_hbm.1, ...), custom_call_target="tpu_custom_call" | custom-call | tf_op jit(solution)/shard_map/pallas_call | solution.py:329
  65.2 2.2 %shard_map.93 = (bf16[16,256]{1,0:T(8,128)(2,1)}, bf16[16,256]{1,0:T(8,128)(2,1)}, bf16[256,896]{1,0:T(8,128)(2,1)}, bf16[256,896]{1,0:T(8,128)(2,1)}, bf16[896,256]{1,0:T(8,128)(2,1)}) custom-call(bf16[16,256]{1,0:T(8,128)(2,1)} %get-tuple-element.10.refs_0_, bf16[16,256]{1,0:T(8,128)(2,1)} %get-tuple-element.11.refs_1_, ...), custom_call_target="tpu_custom_call" | custom-call | tf_op jit(solution)/shard_map/pallas_call | solution.py:354

commit v3 on v2

v3 whole, which is shorter than its diff:
```python
import math

import jax
import jax.numpy as jnp
from jax import lax
from jax.experimental import pallas as pl
from jax.experimental.pallas import tpu as pltpu
from jax.sharding import PartitionSpec as P

MESH = pl.DeviceIdType.MESH
F32 = jnp.float32
BF16 = jnp.bfloat16
RING = 8
ROWS = 16
HALF = RING * ROWS
N_MP = 16
VMEM_LIMIT = 62 * 2**20
CODE_SCALE = float(2**18)


def encode(x):
    x = x * CODE_SCALE
    return (x * x * (x * jnp.abs(x))).astype(BF16)


def decode(code):
    y = code.astype(F32)
    root = lax.rsqrt(lax.rsqrt(jnp.abs(y))) * (1.0 / CODE_SCALE)
    return jnp.where(y < 0, -root, root)


def dot(left, right):
    return jnp.dot(left, right, preferred_element_type=F32)


def dot_last(left, right):
    return lax.dot_general(left, right, (((1,), (1,)), ((), ())), preferred_element_type=F32)


def dot_first(left, right):
    return lax.dot_general(left, right, (((0,), (0,)), ((), ())), preferred_element_type=F32)


def kernel(
    tok_hbm, cot_hbm, wg_hbm, wu_hbm, wd_hbm,
    out_hbm, tgrad_hbm, ggrad_hbm, ugrad_hbm, dgrad_hbm,
    wg, wu, wd, sg, su, sd,
    mine, rows, other, full, acc, send, recv, sendz, recvz,
    hgu, part, parts, small, ggrad, ugrad, dgrad,
    load_sem, mine_sem, wsib_ss, wsib_rs, gat_ss, gat_rs, oth_ss, oth_rs,
    rs_ss, rs_rs, z_ss, z_rs, ag_ss, ag_rs, half_ss, half_rs, o_ss, o_rs, res_sem,
):
    dp, mp = lax.axis_index("dp"), lax.axis_index("mp")
    core, y, zh = dp % 2, (dp // 2) % RING, dp // 16
    rot = mp % RING
    row_core = mp // RING
    sib = (dp + 1 - 2 * core, mp)
    zother = ((1 - zh) * 16 + y * 2 + core, mp)
    factor = 1.0 / math.sqrt(ROWS * N_MP)

    def remote(src, dst, ss, rs, to):
        return pltpu.make_async_remote_copy(
            src_ref=src, dst_ref=dst, send_sem=ss, recv_sem=rs,
            device_id=to, device_id_type=MESH,
        )

    def await_copy(ref, sem):
        pltpu.make_async_copy(ref, ref, sem).wait()

    def along_y(hops):
        return (zh * 16 + ((y + hops + RING) % RING) * 2 + core, mp)

    def local_block(ring_index):
        return (ring_index + 2 * RING + rot) % RING

    def rows16(index):
        return pl.ds(pl.multiple_of(index * ROWS, ROWS), ROWS)

    started = []

    def start(copy):
        copy.start()
        started.append(copy)
        return copy

    own_loads = [
        pltpu.make_async_copy(src, mine.at[i], mine_sem.at[i])
        for i, src in enumerate((tok_hbm, cot_hbm))
    ]
    for copy in own_loads:
        copy.start()
    loads = [
        pltpu.make_async_copy(src, dst, load_sem.at[i])
        for i, (src, dst) in enumerate(((wg_hbm, wg), (wu_hbm, wu), (wd_hbm, wd)))
    ]
    for copy in loads:
        copy.start()

    peers = [sib, zother] + [along_y(hops) for hops in (1, -1, 2, -2)]
    for k in range(1, N_MP):
        peers += [(dp, (mp + k) % N_MP), (sib[0], (mp + k) % N_MP)]
    barrier = pltpu.get_barrier_semaphore()
    for to in peers:
        pl.semaphore_signal(barrier, inc=1, device_id=to, device_id_type=MESH)
    pl.semaphore_wait(barrier, len(peers))

    worker = dp - core + row_core
    at_home = row_core == core
    for copy in own_loads:
        copy.wait()
    target = rows.at[core, rot]
    for k in range(1, N_MP):
        start(
            remote(
                mine, target, gat_ss.at[k], gat_rs.at[core, rot],
                (worker, (mp + k) % N_MP),
            )
        )
    stay = pltpu.make_async_copy(mine, target, gat_rs.at[core, rot])
    cross = remote(mine, target, gat_ss.at[0], gat_rs.at[core, rot], sib)
    pl.when(at_home)(stay.start)
    pl.when(jnp.logical_not(at_home))(cross.start)
    for j, (src, dst) in enumerate(((wg_hbm, sg), (wu_hbm, su), (wd_hbm, sd))):
        start(remote(src, dst, wsib_ss.at[j], wsib_rs.at[j], sib))

    for copy in loads:
        copy.wait()
    for j, dst in enumerate((sg, su, sd)):
        await_copy(dst, wsib_rs.at[j])
    for side in range(2):
        for b in range(RING):
            await_copy(rows.at[side, b], gat_rs.at[side, b])
    near = rows[core].reshape(RING, 2, ROWS, -1)
    far = rows[1 - core].reshape(RING, 2, ROWS, -1)
    near_tok, near_cot = near[:, 0].reshape(HALF, -1), near[:, 1].reshape(HALF, -1)
    far_tok, far_cot = far[:, 0].reshape(HALF, -1), far[:, 1].reshape(HALF, -1)
    acc[0] = dot(near_tok, wg[...]) + dot(far_tok, sg[...])
    acc[1] = dot(near_tok, wu[...]) + dot(far_tok, su[...])
    acc[2] = dot_last(near_cot, wd[...]) + dot_last(far_cot, sd[...])

    def block_sum(hops):
        return acc[:, rows16(local_block(y + hops)), :]

    def send_sums(slot, lane, arrays, hops):
        start(
            remote(
                send.at[slot, arrays], recv.at[slot, arrays],
                rs_ss.at[lane], rs_rs.at[lane], along_y(hops),
            )
        )

    first, rest, whole = pl.ds(0, 1), pl.ds(1, 2), pl.ds(0, 3)
    send[0] = encode(block_sum(4))
    send_sums(0, 0, first, -2)
    send_sums(0, 1, rest, 2)
    send[1] = encode(block_sum(3))
    send_sums(1, 2, whole, 1)
    send[2] = encode(block_sum(-3))
    send_sums(2, 3, whole, -1)
    send[3] = encode(block_sum(1))
    send_sums(3, 4, whole, 1)
    send[4] = encode(block_sum(-1))
    send_sums(4, 5, whole, -1)
    start(remote(rows.at[1 - core], other, oth_ss, oth_rs, sib))
    await_copy(recv.at[1], rs_rs.at[2])
    await_copy(recv.at[0, rest], rs_rs.at[1])
    acc[:, rows16(local_block(y + 2)), :] += decode(recv[1])
    send[5, 0] = encode(acc[0, rows16(local_block(y + 2)), :])
    send[5, 1:] = encode(acc[1:, rows16(local_block(y + 2)), :] + decode(recv[0, 1:]))
    send_sums(5, 6, whole, 2)
    await_copy(recv.at[2], rs_rs.at[3])
    await_copy(recv.at[0, first], rs_rs.at[0])
    acc[:, rows16(local_block(y - 2)), :] += decode(recv[2])
    send[6, 0] = encode(acc[0, rows16(local_block(y - 2)), :] + decode(recv[0, 0]))
    send[6, 1:] = encode(acc[1:, rows16(local_block(y - 2)), :])
    send_sums(6, 7, whole, -2)
    total = block_sum(0)
    for slot, lane in ((3, 4), (4, 5), (5, 6), (6, 7)):
        await_copy(recv.at[slot], rs_rs.at[lane])
        total += decode(recv[slot])
    sendz[...] = encode(total)
    start(remote(sendz, recvz, z_ss, z_rs, zother))
    await_copy(recvz, z_rs)
    total += decode(recvz[...])
    gate, up, grad_hidden = total[0], total[1], total[2]
    sig = jax.nn.sigmoid(gate)

    def block_of(hops):
        return core * RING + local_block(y - hops)

    own = block_of(0)
    hgu[own, 0] = (gate * sig * up).astype(BF16)
    hgu[own, 1] = (grad_hidden * up * sig * (1.0 + gate * (1.0 - sig))).astype(BF16)
    hgu[own, 2] = (grad_hidden * gate * sig).astype(BF16)

    def spread(lane, arrays, source, hops):
        ref = hgu.at[block_of(source), arrays]
        start(remote(ref, ref, ag_ss.at[lane], ag_rs.at[lane], along_y(hops)))

    def arrive(lane, arrays, source):
        await_copy(hgu.at[block_of(source), arrays], ag_rs.at[lane])

    spread(0, whole, 0, 2)
    spread(1, whole, 0, -2)
    spread(2, whole, 0, 1)
    spread(3, whole, 0, -1)
    arrive(0, whole, 2)
    spread(4, whole, 2, 1)
    spread(6, first, 2, 2)
    arrive(1, whole, -2)
    spread(5, whole, -2, -1)
    spread(7, rest, -2, -2)
    arrive(2, whole, 1)
    arrive(3, whole, -1)

    finals = []

    def multiply(batch):
        blocks = [hgu[block_of(hops)] for hops in batch]
        hidden, grad_gate, grad_up = (
            jnp.concatenate([block[array] for block in blocks], axis=0) for array in range(3)
        )
        for side, (gate_w, up_w, down_w) in enumerate(((wg, wu, wd), (sg, su, sd))):
            values = (
                dot(hidden, down_w[...]),
                dot_last(grad_gate, gate_w[...]) + dot_last(grad_up, up_w[...]),
            )
            for n, hops in enumerate(batch):
                slot = (hops + RING) % RING * 2 + side
                index = block_of(hops)
                for which in range(2):
                    value = values[which][n * ROWS : (n + 1) * ROWS]
                    part[slot, which] = value.astype(BF16)
                src, dst = part.at[slot], parts.at[mp]
                copy = remote(
                    src, dst, o_ss.at[slot], o_rs.at[mp], (sib[0] if side else dp, index)
                )
                if side == 0:
                    stay = pltpu.make_async_copy(src, dst, o_rs.at[mp])
                    pl.when(index == mp)(stay.start)
                    pl.when(index != mp)(copy.start)
                    finals.append((copy, index))
                else:
                    start(copy)

    multiply((0, 1, -1, 2, -2))
    arrive(4, whole, 3)
    arrive(5, whole, -3)
    arrive(6, first, 4)
    arrive(7, rest, -4)
    multiply((3, -3, 4))

    my_half = hgu.at[pl.ds(pl.multiple_of(core * RING, RING), RING)]
    their_half = hgu.at[pl.ds(pl.multiple_of((1 - core) * RING, RING), RING)]
    start(remote(my_half, my_half, half_ss, half_rs, sib))
    await_copy(other, oth_rs)
    theirs = other[...]
    for i in range(2):
        full[i, pl.ds(pl.multiple_of(core * HALF, HALF), HALF), :] = (
            rows[core][:, i].reshape(HALF, -1)
        )
        full[i, pl.ds(pl.multiple_of((1 - core) * HALF, HALF), HALF), :] = (
            theirs[:, i].reshape(HALF, -1)
        )

    results = []

    def store(src, dst):
        copy = pltpu.make_async_copy(src, dst, res_sem.at[len(results)])
        copy.start()
        results.append(copy)

    await_copy(their_half, half_rs)
    hidden = hgu[:, 0].reshape(2 * HALF, -1)
    grad_gate = hgu[:, 1].reshape(2 * HALF, -1)
    grad_up = hgu[:, 2].reshape(2 * HALF, -1)
    ggrad[...] = (dot_first(full[0], grad_gate) * factor).astype(BF16)
    store(ggrad, ggrad_hbm)
    ugrad[...] = (dot_first(full[0], grad_up) * factor).astype(BF16)
    store(ugrad, ugrad_hbm)
    dgrad[...] = (dot_first(hidden, full[1]) * factor).astype(BF16)
    store(dgrad, dgrad_hbm)

    total = jnp.zeros((2, ROWS, 256), F32)
    for k in range(N_MP):
        await_copy(parts.at[k], o_rs.at[k])
        total += parts[k].astype(F32)
    small[...] = total.astype(BF16)
    store(small.at[0], out_hbm)
    store(small.at[1], tgrad_hbm)

    for copy in started:
        copy.wait_send()
    pl.when(jnp.logical_not(at_home))(cross.wait_send)
    for copy, index in finals:
        pl.when(index != mp)(copy.wait_send)
    for copy in results:
        copy.wait()


def copy_out(*refs):
    sources, targets, staged, sems = refs[:5], refs[5:10], refs[10:15], refs[15]
    loads = [
        pltpu.make_async_copy(src, mid, sems.at[0, i])
        for i, (src, mid) in enumerate(zip(sources, staged))
    ]
    stores = [
        pltpu.make_async_copy(mid, dst, sems.at[1, i])
        for i, (mid, dst) in enumerate(zip(staged, targets))
    ]
    for copy in loads:
        copy.start()
    for load, store in zip(loads, stores):
        load.wait()
        store.start()
    for copy in stores:
        copy.wait()


def on_device(tokens, gate_weight, up_weight, down_weight, cotangent):
    count, width = tokens.shape
    units = gate_weight.shape[1]
    hbm = pl.BlockSpec(memory_space=pltpu.HBM)
    dma = pltpu.SemaphoreType.DMA

    def vmem(*shape, dtype=BF16):
        return pltpu.VMEM(shape, dtype)

    shapes = (
        jax.ShapeDtypeStruct((count, width), BF16),
        jax.ShapeDtypeStruct((count, width), BF16),
        jax.ShapeDtypeStruct((width, units), BF16),
        jax.ShapeDtypeStruct((width, units), BF16),
        jax.ShapeDtypeStruct((units, width), BF16),
    )
    results = pl.pallas_call(
        kernel,
        out_shape=shapes,
        in_specs=[hbm] * 5,
        out_specs=[hbm] * 5,
        scratch_shapes=[
            vmem(width, units), vmem(width, units), vmem(units, width),
            vmem(width, units), vmem(width, units), vmem(units, width),
            vmem(2, ROWS, width), vmem(2, RING, 2, ROWS, width), vmem(RING, 2, ROWS, width),
            vmem(2, 2 * HALF, width), vmem(3, HALF, units, dtype=F32),
            vmem(7, 3, ROWS, units), vmem(7, 3, ROWS, units),
            vmem(3, ROWS, units), vmem(3, ROWS, units),
            vmem(N_MP, 3, ROWS, units),
            vmem(N_MP, 2, ROWS, width), vmem(N_MP, 2, ROWS, width), vmem(2, ROWS, width),
            vmem(width, units), vmem(width, units), vmem(units, width),
            dma((3,)), dma((2,)), dma((3,)), dma((3,)), dma((N_MP,)), dma((2, RING)),
            dma(()), dma(()), dma((8,)), dma((8,)), dma(()), dma(()),
            dma((8,)), dma((8,)), dma(()), dma(()), dma((N_MP,)), dma((N_MP,)), dma((5,)),
        ],
        compiler_params=pltpu.CompilerParams(
            collective_id=0, has_side_effects=True, vmem_limit_bytes=VMEM_LIMIT
        ),
    )(tokens, cotangent, gate_weight, up_weight, down_weight)
    return pl.pallas_call(
        copy_out,
        out_shape=shapes,
        in_specs=[hbm] * 5,
        out_specs=[hbm] * 5,
        scratch_shapes=[pltpu.VMEM(s.shape, s.dtype) for s in shapes] + [dma((2, 5))],
        compiler_params=pltpu.CompilerParams(vmem_limit_bytes=VMEM_LIMIT),
    )(*results)


def solution(mesh):
    in_specs = (P("mp", "dp"), P("dp", "mp"), P("dp", "mp"), P("mp", "dp"), P("mp", "dp"))
    out_specs = (P("mp", "dp"), P("mp", "dp"), P("dp", "mp"), P("dp", "mp"), P("mp", "dp"))
    return jax.shard_map(
        on_device, mesh=mesh, in_specs=in_specs, out_specs=out_specs, check_vma=False
    )
```

time: 67.6 us -> 65.1 us (0.963)
  Pallas kernels: 66.7 us -> 64.3 us
    pallas_call x1, Pallas kernels: 64.5 us -> 62.1 us  [on_device(): pl.pallas_call(kernel, out_shape=shapes, in_specs=[hbm] * 5, out_specs=[h...]
where the time goes in v3:
time: 65.1 us; the launch traced here: 64.9 us
  Pallas kernels  64.3 us (99%)
    pallas_call x1, Pallas kernels, on_device(): pl.pallas_call(kernel, out_shape=shapes, in_specs=[hbm] * 5, out_specs=[h...  62.1 us
    pallas_call x1, Pallas kernels, on_device(): pl.pallas_call(copy_out, out_shape=shapes, in_specs=[hbm] * 5, out_specs=...  2.21 us

profile of v3, /device:TPU:1, one launch (start us, length us, event | category | flops | bytes accessed | tf_op | source)
XLA Modules:
  0.0 64.9 jit_solution(14637551076377071964)
XLA Ops:
  0.6 62.1 %shard_map.92 = (bf16[16,256]{1,0:T(8,128)(2,1)}, bf16[16,256]{1,0:T(8,128)(2,1)}, bf16[256,896]{1,0:T(8,128)(2,1)}, bf16[256,896]{1,0:T(8,128)(2,1)}, bf16[896,256]{1,0:T(8,128)(2,1)}) custom-call(bf16[16,256]{1,0:T(8,128)(2,1)} %tok_hbm.1, bf16[16,256]{1,0:T(8,128)(2,1)} %cot_hbm.1, bf16[256,896]{1,0:T(8,128)(2,1)} %wg_hbm.1, bf16[256,896]{1,0:T(8,128)(2,1)} %wu_hbm.1, ...), custom_call_target="tpu_custom_call" | custom-call | tf_op jit(solution)/shard_map/pallas_call | solution.py:336
  62.7 2.2 %shard_map.93 = (bf16[16,256]{1,0:T(8,128)(2,1)}, bf16[16,256]{1,0:T(8,128)(2,1)}, bf16[256,896]{1,0:T(8,128)(2,1)}, bf16[256,896]{1,0:T(8,128)(2,1)}, bf16[896,256]{1,0:T(8,128)(2,1)}) custom-call(bf16[16,256]{1,0:T(8,128)(2,1)} %get-tuple-element.10.refs_0_, bf16[16,256]{1,0:T(8,128)(2,1)} %get-tuple-element.11.refs_1_, ...), custom_call_target="tpu_custom_call" | custom-call | tf_op jit(solution)/shard_map/pallas_call | solution.py:359

commit v4 on v3

--- a/solution.py
+++ b/solution.py
@@ -138,80 +138,82 @@
     acc[1] = dot(near_tok, wu[...]) + dot(far_tok, su[...])
     acc[2] = dot_last(near_cot, wd[...]) + dot_last(far_cot, sd[...])
 
-    def block_sum(hops):
-        return acc[:, rows16(local_block(y + hops)), :]
-
-    def send_sums(slot, lane, arrays, hops):
+    def block_sum(array, hops):
+        return acc[array, rows16(local_block(y + hops)), :]
+
+    def send_sums(slot, array, value, hops):
+        send[slot, array] = encode(value)
         start(
             remote(
-                send.at[slot, arrays], recv.at[slot, arrays],
-                rs_ss.at[lane], rs_rs.at[lane], along_y(hops),
+                send.at[slot, array], recv.at[slot, array],
+                rs_ss.at[slot, array], rs_rs.at[slot, array], along_y(hops),
             )
         )
 
-    first, rest, whole = pl.ds(0, 1), pl.ds(1, 2), pl.ds(0, 3)
-    send[0] = encode(block_sum(4))
-    send_sums(0, 0, first, -2)
-    send_sums(0, 1, rest, 2)
-    send[1] = encode(block_sum(3))
-    send_sums(1, 2, whole, 1)
-    send[2] = encode(block_sum(-3))
-    send_sums(2, 3, whole, -1)
-    send[3] = encode(block_sum(1))
-    send_sums(3, 4, whole, 1)
-    send[4] = encode(block_sum(-1))
-    send_sums(4, 5, whole, -1)
+    def received(slot, array):
+        await_copy(recv.at[slot, array], rs_rs.at[slot, array])
+        return decode(recv[slot, array])
+
+    far_side = (-2, 2, 2)
+    for array in range(3):
+        send_sums(0, array, block_sum(array, 4), far_side[array])
+        send_sums(1, array, block_sum(array, 3), 1)
+        send_sums(2, array, block_sum(array, -3), -1)
+    for array in range(3):
+        send_sums(3, array, block_sum(array, 1), 1)
+        send_sums(4, array, block_sum(array, -1), -1)
+    for array in range(3):
+        for slot, hops in ((1, 2), (2, -2)):
+            value = block_sum(array, hops) + received(slot, array)
+            if far_side[array] == hops:
+                value += received(0, array)
+            send_sums(slot + 4, array, value, hops)
     start(remote(rows.at[1 - core], other, oth_ss, oth_rs, sib))
-    await_copy(recv.at[1], rs_rs.at[2])
-    await_copy(recv.at[0, rest], rs_rs.at[1])
-    acc[:, rows16(local_block(y + 2)), :] += decode(recv[1])
-    send[5, 0] = encode(acc[0, rows16(local_block(y + 2)), :])
-    send[5, 1:] = encode(acc[1:, rows16(local_block(y + 2)), :] + decode(recv[0, 1:]))
-    send_sums(5, 6, whole, 2)
-    await_copy(recv.at[2], rs_rs.at[3])
-    await_copy(recv.at[0, first], rs_rs.at[0])
-    acc[:, rows16(local_block(y - 2)), :] += decode(recv[2])
-    send[6, 0] = encode(acc[0, rows16(local_block(y - 2)), :] + decode(recv[0, 0]))
-    send[6, 1:] = encode(acc[1:, rows16(local_block(y - 2)), :])
-    send_sums(6, 7, whole, -2)
-    total = block_sum(0)
-    for slot, lane in ((3, 4), (4, 5), (5, 6), (6, 7)):
-        await_copy(recv.at[slot], rs_rs.at[lane])
-        total += decode(recv[slot])
-    sendz[...] = encode(total)
-    start(remote(sendz, recvz, z_ss, z_rs, zother))
-    await_copy(recvz, z_rs)
-    total += decode(recvz[...])
-    gate, up, grad_hidden = total[0], total[1], total[2]
-    sig = jax.nn.sigmoid(gate)
+    totals = []
+    for array in range(3):
+        total = block_sum(array, 0)
+        for slot in (3, 4, 5, 6):
+            total += received(slot, array)
+        sendz[array] = encode(total)
+        start(remote(sendz.at[array], recvz.at[array], z_ss.at[array], z_rs.at[array], zother))
+        totals.append(total)
+
+    def swapped(array):
+        await_copy(recvz.at[array], z_rs.at[array])
+        return totals[array] + decode(recvz[array])
 
     def block_of(hops):
         return core * RING + local_block(y - hops)
 
+    groups = (slice(0, 1), slice(1, 3))
+
+    def spread(lane, group, source, hops):
+        ref = hgu.at[block_of(source), groups[group]]
+        start(remote(ref, ref, ag_ss.at[lane, group], ag_rs.at[lane, group], along_y(hops)))
+
+    def arrive(lane, group, source):
+        await_copy(hgu.at[block_of(source), groups[group]], ag_rs.at[lane, group])
+
     own = block_of(0)
+    gate, up = swapped(0), swapped(1)
+    sig = jax.nn.sigmoid(gate)
     hgu[own, 0] = (gate * sig * up).astype(BF16)
+    for lane, hops in enumerate((2, -2, 1, -1)):
+        spread(lane, 0, 0, hops)
+    grad_hidden = swapped(2)
     hgu[own, 1] = (grad_hidden * up * sig * (1.0 + gate * (1.0 - sig))).astype(BF16)
     hgu[own, 2] = (grad_hidden * gate * sig).astype(BF16)
-
-    def spread(lane, arrays, source, hops):
-        ref = hgu.at[block_of(source), arrays]
-        start(remote(ref, ref, ag_ss.at[lane], ag_rs.at[lane], along_y(hops)))
-
-    def arrive(lane, arrays, source):
-        await_copy(hgu.at[block_of(source), arrays], ag_rs.at[lane])
-
-    spread(0, whole, 0, 2)
-    spread(1, whole, 0, -2)
-    spread(2, whole, 0, 1)
-    spread(3, whole, 0, -1)
-    arrive(0, whole, 2)
-    spread(4, whole, 2, 1)
-    spread(6, first, 2, 2)
-    arrive(1, whole, -2)
-    spread(5, whole, -2, -1)
-    spread(7, rest, -2, -2)
-    arrive(2, whole, 1)
-    arrive(3, whole, -1)
+    for lane, hops in enumerate((2, -2, 1, -1)):
+        spread(lane, 1, 0, hops)
+    for group in range(2):
+        for lane, hops in ((0, 2), (1, -2)):
+            arrive(lane, group, hops)
+            spread(lane + 4, group, hops, hops // 2)
+            if (hops > 0) == (group == 0):
+                spread(6, group, hops, hops)
+    for group in range(2):
+        arrive(2, group, 1)
+        arrive(3, group, -1)
 
     finals = []
 
@@ -244,10 +246,10 @@
                     start(copy)
 
     multiply((0, 1, -1, 2, -2))
-    arrive(4, whole, 3)
-    arrive(5, whole, -3)
-    arrive(6, first, 4)
-    arrive(7, rest, -4)
+    for group in range(2):
+        arrive(4, group, 3)
+        arrive(5, group, -3)
+        arrive(6, group, 4)
     multiply((3, -3, 4))
 
     my_half = hgu.at[pl.ds(pl.multiple_of(core * RING, RING), RING)]
@@ -349,8 +351,8 @@
             vmem(N_MP, 2, ROWS, width), vmem(N_MP, 2, ROWS, width), vmem(2, ROWS, width),
             vmem(width, units), vmem(width, units), vmem(units, width),
             dma((3,)), dma((2,)), dma((3,)), dma((3,)), dma((N_MP,)), dma((2, RING)),
-            dma(()), dma(()), dma((8,)), dma((8,)), dma(()), dma(()),
-            dma((8,)), dma((8,)), dma(()), dma(()), dma((N_MP,)), dma((N_MP,)), dma((5,)),
+            dma(()), dma(()), dma((7, 3)), dma((7, 3)), dma((3,)), dma((3,)),
+            dma((7, 2)), dma((7, 2)), dma(()), dma(()), dma((N_MP,)), dma((N_MP,)), dma((5,)),
         ],
         compiler_params=pltpu.CompilerParams(
             collective_id=0, has_side_effects=True, vmem_limit_bytes=VMEM_LIMIT

time: 65.1 us -> 62.4 us (0.959)
  Pallas kernels: 64.3 us -> 61.5 us
    pallas_call x1, Pallas kernels: 62.1 us -> 59.3 us  [on_device(): pl.pallas_call(kernel, out_shape=shapes, in_specs=[hbm] * 5, out_specs=[h...]
where the time goes in v4:
time: 62.4 us; the launch traced here: 62.2 us
  Pallas kernels  61.5 us (99%)
  between operations  0.64 us (1%)
    pallas_call x1, Pallas kernels, on_device(): pl.pallas_call(kernel, out_shape=shapes, in_specs=[hbm] * 5, out_specs=[h...  59.3 us
    pallas_call x1, Pallas kernels, on_device(): pl.pallas_call(copy_out, out_shape=shapes, in_specs=[hbm] * 5, out_specs=...  2.21 us

profile of v4, /device:TPU:1, one launch (start us, length us, event | category | flops | bytes accessed | tf_op | source)
XLA Modules:
  0.0 62.2 jit_solution(12036288145626207378)
XLA Ops:
  0.6 59.3 %shard_map.92 = (bf16[16,256]{1,0:T(8,128)(2,1)}, bf16[16,256]{1,0:T(8,128)(2,1)}, bf16[256,896]{1,0:T(8,128)(2,1)}, bf16[256,896]{1,0:T(8,128)(2,1)}, bf16[896,256]{1,0:T(8,128)(2,1)}) custom-call(bf16[16,256]{1,0:T(8,128)(2,1)} %tok_hbm.1, bf16[16,256]{1,0:T(8,128)(2,1)} %cot_hbm.1, bf16[256,896]{1,0:T(8,128)(2,1)} %wg_hbm.1, bf16[256,896]{1,0:T(8,128)(2,1)} %wu_hbm.1, ...), custom_call_target="tpu_custom_call" | custom-call | tf_op jit(solution)/shard_map/pallas_call | solution.py:338
  60.0 2.2 %shard_map.93 = (bf16[16,256]{1,0:T(8,128)(2,1)}, bf16[16,256]{1,0:T(8,128)(2,1)}, bf16[256,896]{1,0:T(8,128)(2,1)}, bf16[256,896]{1,0:T(8,128)(2,1)}, bf16[896,256]{1,0:T(8,128)(2,1)}) custom-call(bf16[16,256]{1,0:T(8,128)(2,1)} %get-tuple-element.10.refs_0_, bf16[16,256]{1,0:T(8,128)(2,1)} %get-tuple-element.11.refs_1_, ...), custom_call_target="tpu_custom_call" | custom-call | tf_op jit(solution)/shard_map/pallas_call | solution.py:361

commit v5 on v4

--- a/solution.py
+++ b/solution.py
@@ -96,30 +96,40 @@
     for copy in loads:
         copy.start()
 
-    peers = [sib, zother] + [along_y(hops) for hops in (1, -1, 2, -2)]
-    for k in range(1, N_MP):
-        peers += [(dp, (mp + k) % N_MP), (sib[0], (mp + k) % N_MP)]
-    barrier = pltpu.get_barrier_semaphore()
-    for to in peers:
-        pl.semaphore_signal(barrier, inc=1, device_id=to, device_id_type=MESH)
-    pl.semaphore_wait(barrier, len(peers))
-
     worker = dp - core + row_core
     at_home = row_core == core
-    for copy in own_loads:
-        copy.wait()
-    target = rows.at[core, rot]
-    for k in range(1, N_MP):
-        start(
-            remote(
-                mine, target, gat_ss.at[k], gat_rs.at[core, rot],
-                (worker, (mp + k) % N_MP),
-            )
-        )
-    stay = pltpu.make_async_copy(mine, target, gat_rs.at[core, rot])
-    cross = remote(mine, target, gat_ss.at[0], gat_rs.at[core, rot], sib)
-    pl.when(at_home)(stay.start)
-    pl.when(jnp.logical_not(at_home))(cross.start)
+    peers = [zother] + [along_y(hops) for hops in (1, -1, 2, -2)]
+    peers += [(worker, (mp + k) % N_MP) for k in range(1, N_MP)]
+    idle = dp - core + 1 - row_core
+    peers += [(idle, core * RING + (rot + k) % RING) for k in range(1, RING)]
+    barrier = pltpu.get_barrier_semaphore()
+
+    def greet(to):
+        pl.semaphore_signal(barrier, inc=1, device_id=to, device_id_type=MESH)
+
+    for to in peers:
+        greet(to)
+    greet(sib)
+    away = jnp.where(at_home, 0, 1)
+    pl.when(jnp.logical_not(at_home))(lambda: greet((idle, core * RING + rot)))
+    pl.semaphore_wait(barrier, len(peers) + 1 + away)
+
+    z_lo, x = mp // 4, mp % 4
+    crossings = []
+    for i in range(2):
+        own_loads[i].wait()
+        source, target = mine.at[i], rows.at[core, i, rot]
+        arrived = gat_rs.at[i, core, rot]
+        for k, z_to in enumerate((3 - z_lo, (z_lo + 2) % 4, z_lo + 1 - 2 * (z_lo % 2), z_lo)):
+            for n, x_step in enumerate((2, 1, 3, 0)):
+                if k < 3 or x_step:
+                    to = (worker, z_to * 4 + (x + x_step) % 4)
+                    start(remote(source, target, gat_ss.at[i, 4 * k + n], arrived, to))
+        stay = pltpu.make_async_copy(source, target, arrived)
+        cross = remote(source, target, gat_ss.at[i, 15], arrived, sib)
+        pl.when(at_home)(stay.start)
+        pl.when(jnp.logical_not(at_home))(cross.start)
+        crossings.append(cross)
     for j, (src, dst) in enumerate(((wg_hbm, sg), (wu_hbm, su), (wd_hbm, sd))):
         start(remote(src, dst, wsib_ss.at[j], wsib_rs.at[j], sib))
 
@@ -127,16 +137,12 @@
         copy.wait()
     for j, dst in enumerate((sg, su, sd)):
         await_copy(dst, wsib_rs.at[j])
-    for side in range(2):
-        for b in range(RING):
-            await_copy(rows.at[side, b], gat_rs.at[side, b])
-    near = rows[core].reshape(RING, 2, ROWS, -1)
-    far = rows[1 - core].reshape(RING, 2, ROWS, -1)
-    near_tok, near_cot = near[:, 0].reshape(HALF, -1), near[:, 1].reshape(HALF, -1)
-    far_tok, far_cot = far[:, 0].reshape(HALF, -1), far[:, 1].reshape(HALF, -1)
-    acc[0] = dot(near_tok, wg[...]) + dot(far_tok, sg[...])
-    acc[1] = dot(near_tok, wu[...]) + dot(far_tok, su[...])
-    acc[2] = dot_last(near_cot, wd[...]) + dot_last(far_cot, sd[...])
+
+    def arrived_rows(i):
+        for side in range(2):
+            for b in range(RING):
+                await_copy(rows.at[side, i, b], gat_rs.at[i, side, b])
+        return rows[core, i].reshape(HALF, -1), rows[1 - core, i].reshape(HALF, -1)
 
     def block_sum(array, hops):
         return acc[array, rows16(local_block(y + hops)), :]
@@ -155,13 +161,23 @@
         return decode(recv[slot, array])
 
     far_side = (-2, 2, 2)
-    for array in range(3):
-        send_sums(0, array, block_sum(array, 4), far_side[array])
-        send_sums(1, array, block_sum(array, 3), 1)
-        send_sums(2, array, block_sum(array, -3), -1)
-    for array in range(3):
-        send_sums(3, array, block_sum(array, 1), 1)
-        send_sums(4, array, block_sum(array, -1), -1)
+
+    def send_terms(arrays):
+        for array in arrays:
+            send_sums(0, array, block_sum(array, 4), far_side[array])
+            send_sums(1, array, block_sum(array, 3), 1)
+            send_sums(2, array, block_sum(array, -3), -1)
+        for array in arrays:
+            send_sums(3, array, block_sum(array, 1), 1)
+            send_sums(4, array, block_sum(array, -1), -1)
+
+    near, far = arrived_rows(0)
+    acc[0] = dot(near, wg[...]) + dot(far, sg[...])
+    acc[1] = dot(near, wu[...]) + dot(far, su[...])
+    send_terms((0, 1))
+    near, far = arrived_rows(1)
+    acc[2] = dot_last(near, wd[...]) + dot_last(far, sd[...])
+    send_terms((2,))
     for array in range(3):
         for slot, hops in ((1, 2), (2, -2)):
             value = block_sum(array, hops) + received(slot, array)
@@ -185,7 +201,7 @@
     def block_of(hops):
         return core * RING + local_block(y - hops)
 
-    groups = (slice(0, 1), slice(1, 3))
+    groups = (slice(0, 1), slice(1, 2), slice(2, 3))
 
     def spread(lane, group, source, hops):
         ref = hgu.at[block_of(source), groups[group]]
@@ -202,67 +218,79 @@
         spread(lane, 0, 0, hops)
     grad_hidden = swapped(2)
     hgu[own, 1] = (grad_hidden * up * sig * (1.0 + gate * (1.0 - sig))).astype(BF16)
+    for lane, hops in enumerate((2, -2)):
+        spread(lane, 1, 0, hops)
     hgu[own, 2] = (grad_hidden * gate * sig).astype(BF16)
-    for lane, hops in enumerate((2, -2, 1, -1)):
-        spread(lane, 1, 0, hops)
-    for group in range(2):
+    for lane, hops in enumerate((2, -2)):
+        spread(lane, 2, 0, hops)
+    for group in (1, 2):
+        for lane, hops in ((2, 1), (3, -1)):
+            spread(lane, group, 0, hops)
+    for group in range(3):
         for lane, hops in ((0, 2), (1, -2)):
             arrive(lane, group, hops)
             spread(lane + 4, group, hops, hops // 2)
-            if (hops > 0) == (group == 0):
+            if hops == far_side[group]:
                 spread(6, group, hops, hops)
-    for group in range(2):
+    for group in range(3):
         arrive(2, group, 1)
         arrive(3, group, -1)
 
     finals = []
 
-    def multiply(batch):
-        blocks = [hgu[block_of(hops)] for hops in batch]
-        hidden, grad_gate, grad_up = (
-            jnp.concatenate([block[array] for block in blocks], axis=0) for array in range(3)
-        )
-        for side, (gate_w, up_w, down_w) in enumerate(((wg, wu, wd), (sg, su, sd))):
-            values = (
-                dot(hidden, down_w[...]),
-                dot_last(grad_gate, gate_w[...]) + dot_last(grad_up, up_w[...]),
-            )
-            for n, hops in enumerate(batch):
-                slot = (hops + RING) % RING * 2 + side
-                index = block_of(hops)
-                for which in range(2):
-                    value = values[which][n * ROWS : (n + 1) * ROWS]
-                    part[slot, which] = value.astype(BF16)
-                src, dst = part.at[slot], parts.at[mp]
-                copy = remote(
-                    src, dst, o_ss.at[slot], o_rs.at[mp], (sib[0] if side else dp, index)
-                )
-                if side == 0:
-                    stay = pltpu.make_async_copy(src, dst, o_rs.at[mp])
-                    pl.when(index == mp)(stay.start)
-                    pl.when(index != mp)(copy.start)
-                    finals.append((copy, index))
-                else:
-                    start(copy)
-
-    multiply((0, 1, -1, 2, -2))
-    for group in range(2):
+    def deliver(which, side, batch, values):
+        for n, hops in enumerate(batch):
+            slot = (hops + RING) % RING * 2 + side
+            index = block_of(hops)
+            part[which, slot] = values[n * ROWS : (n + 1) * ROWS].astype(BF16)
+            src, dst = part.at[which, slot], parts.at[which, mp]
+            sems = o_ss.at[which, slot], o_rs.at[which, mp]
+            copy = remote(src, dst, *sems, (sib[0] if side else dp, index))
+            if side == 0:
+                stay = pltpu.make_async_copy(src, dst, sems[1])
+                pl.when(index == mp)(stay.start)
+                pl.when(index != mp)(copy.start)
+                finals.append((copy, index))
+            else:
+                start(copy)
+
+    def stacked(array, batch):
+        return jnp.concatenate([hgu[block_of(hops), array] for hops in batch], axis=0)
+
+    def multiply_hidden(batch):
+        hidden = stacked(0, batch)
+        for side, down_w in enumerate((wd, sd)):
+            deliver(0, side, batch, dot(hidden, down_w[...]))
+
+    def multiply_grads(batch):
+        grad_gate, grad_up = stacked(1, batch), stacked(2, batch)
+        for side, (gate_w, up_w) in enumerate(((wg, wu), (sg, su))):
+            value = dot_last(grad_gate, gate_w[...]) + dot_last(grad_up, up_w[...])
+            deliver(1, side, batch, value)
+
+    def arrive_far(group):
         arrive(4, group, 3)
         arrive(5, group, -3)
         arrive(6, group, 4)
-    multiply((3, -3, 4))
+
+    multiply_hidden((0, 1, -1, 2, -2))
+    multiply_grads((0, 1, -1, 2, -2))
+    arrive_far(0)
+    multiply_hidden((3, -3, 4))
+    arrive_far(1)
+    arrive_far(2)
+    multiply_grads((3, -3, 4))
 
     my_half = hgu.at[pl.ds(pl.multiple_of(core * RING, RING), RING)]
     their_half = hgu.at[pl.ds(pl.multiple_of((1 - core) * RING, RING), RING)]
     start(remote(my_half, my_half, half_ss, half_rs, sib))
     await_copy(other, oth_rs)
-    theirs = other[...]
     for i in range(2):
         full[i, pl.ds(pl.multiple_of(core * HALF, HALF), HALF), :] = (
-            rows[core][:, i].reshape(HALF, -1)
+            rows[core, i].reshape(HALF, -1)
         )
         full[i, pl.ds(pl.multiple_of((1 - core) * HALF, HALF), HALF), :] = (
-            theirs[:, i].reshape(HALF, -1)
+            other[i].reshape(HALF, -1)
         )
 
     results = []
@@ -283,17 +311,18 @@
     dgrad[...] = (dot_first(hidden, full[1]) * factor).astype(BF16)
     store(dgrad, dgrad_hbm)
 
-    total = jnp.zeros((2, ROWS, 256), F32)
-    for k in range(N_MP):
-        await_copy(parts.at[k], o_rs.at[k])
-        total += parts[k].astype(F32)
-    small[...] = total.astype(BF16)
-    store(small.at[0], out_hbm)
-    store(small.at[1], tgrad_hbm)
+    for which, target in enumerate((out_hbm, tgrad_hbm)):
+        total = jnp.zeros((ROWS, 256), F32)
+        for k in range(N_MP):
+            await_copy(parts.at[which, k], o_rs.at[which, k])
+            total += parts[which, k].astype(F32)
+        small[which] = total.astype(BF16)
+        store(small.at[which], target)
 
     for copy in started:
         copy.wait_send()
-    pl.when(jnp.logical_not(at_home))(cross.wait_send)
+    for cross in crossings:
+        pl.when(jnp.logical_not(at_home))(cross.wait_send)
     for copy, index in finals:
         pl.when(index != mp)(copy.wait_send)
     for copy in results:
@@ -343,16 +372,16 @@
         scratch_shapes=[
             vmem(width, units), vmem(width, units), vmem(units, width),
             vmem(width, units), vmem(width, units), vmem(units, width),
-            vmem(2, ROWS, width), vmem(2, RING, 2, ROWS, width), vmem(RING, 2, ROWS, width),
+            vmem(2, ROWS, width), vmem(2, 2, RING, ROWS, width), vmem(2, RING, ROWS, width),
             vmem(2, 2 * HALF, width), vmem(3, HALF, units, dtype=F32),
             vmem(7, 3, ROWS, units), vmem(7, 3, ROWS, units),
             vmem(3, ROWS, units), vmem(3, ROWS, units),
             vmem(N_MP, 3, ROWS, units),
-            vmem(N_MP, 2, ROWS, width), vmem(N_MP, 2, ROWS, width), vmem(2, ROWS, width),
+            vmem(2, N_MP, ROWS, width), vmem(2, N_MP, ROWS, width), vmem(2, ROWS, width),
             vmem(width, units), vmem(width, units), vmem(units, width),
-            dma((3,)), dma((2,)), dma((3,)), dma((3,)), dma((N_MP,)), dma((2, RING)),
+            dma((3,)), dma((2,)), dma((3,)), dma((3,)), dma((2, N_MP)), dma((2, 2, RING)),
             dma(()), dma(()), dma((7, 3)), dma((7, 3)), dma((3,)), dma((3,)),
-            dma((7, 2)), dma((7, 2)), dma(()), dma(()), dma((N_MP,)), dma((N_MP,)), dma((5,)),
+            dma((7, 3)), dma((7, 3)), dma(()), dma(()), dma((2, N_MP)), dma((2, N_MP)), dma((5,)),
         ],
         compiler_params=pltpu.CompilerParams(
             collective_id=0, has_side_effects=True, vmem_limit_bytes=VMEM_LIMIT

time: 62.4 us -> 60.3 us (0.966)
  Pallas kernels: 61.5 us -> 59.5 us
    pallas_call x1, Pallas kernels: 59.3 us -> 57.2 us  [on_device(): pl.pallas_call(kernel, out_shape=shapes, in_specs=[hbm] * 5, out_specs=[h...]
where the time goes in v5:
time: 60.3 us; the launch traced here: 60.1 us
  Pallas kernels  59.5 us (99%)
  between operations  0.64 us (1%)
    pallas_call x1, Pallas kernels, on_device(): pl.pallas_call(kernel, out_shape=shapes, in_specs=[hbm] * 5, out_specs=[h...  57.2 us
    pallas_call x1, Pallas kernels, on_device(): pl.pallas_call(copy_out, out_shape=shapes, in_specs=[hbm] * 5, out_specs=...  2.21 us

profile of v5, /device:TPU:1, one launch (start us, length us, event | category | flops | bytes accessed | tf_op | source)
XLA Modules:
  0.0 60.1 jit_solution(17329354520758408573)
XLA Ops:
  0.6 57.2 %shard_map.92 = (bf16[16,256]{1,0:T(8,128)(2,1)}, bf16[16,256]{1,0:T(8,128)(2,1)}, bf16[256,896]{1,0:T(8,128)(2,1)}, bf16[256,896]{1,0:T(8,128)(2,1)}, bf16[896,256]{1,0:T(8,128)(2,1)}) custom-call(bf16[16,256]{1,0:T(8,128)(2,1)} %tok_hbm.1, bf16[16,256]{1,0:T(8,128)(2,1)} %cot_hbm.1, bf16[256,896]{1,0:T(8,128)(2,1)} %wg_hbm.1, bf16[256,896]{1,0:T(8,128)(2,1)} %wu_hbm.1, ...), custom_call_target="tpu_custom_call" | custom-call | tf_op jit(solution)/shard_map/pallas_call | solution.py:367
  57.9 2.2 %shard_map.93 = (bf16[16,256]{1,0:T(8,128)(2,1)}, bf16[16,256]{1,0:T(8,128)(2,1)}, bf16[256,896]{1,0:T(8,128)(2,1)}, bf16[256,896]{1,0:T(8,128)(2,1)}, bf16[896,256]{1,0:T(8,128)(2,1)}) custom-call(bf16[16,256]{1,0:T(8,128)(2,1)} %get-tuple-element.10.refs_0_, bf16[16,256]{1,0:T(8,128)(2,1)} %get-tuple-element.11.refs_1_, ...), custom_call_target="tpu_custom_call" | custom-call | tf_op jit(solution)/shard_map/pallas_call | solution.py:390

commit v6 on v5

--- a/solution.py
+++ b/solution.py
@@ -130,13 +130,10 @@
         pl.when(at_home)(stay.start)
         pl.when(jnp.logical_not(at_home))(cross.start)
         crossings.append(cross)
-    for j, (src, dst) in enumerate(((wg_hbm, sg), (wu_hbm, su), (wd_hbm, sd))):
-        start(remote(src, dst, wsib_ss.at[j], wsib_rs.at[j], sib))
-
-    for copy in loads:
-        copy.wait()
-    for j, dst in enumerate((sg, su, sd)):
-        await_copy(dst, wsib_rs.at[j])
+        for j in ((0, 1), (2,))[i]:
+            src, dst = ((wg_hbm, sg), (wu_hbm, su), (wd_hbm, sd))[j]
+            start(remote(src, dst, wsib_ss.at[j], wsib_rs.at[j], sib))
+
 
     def arrived_rows(i):
         for side in range(2):
@@ -162,22 +159,29 @@
 
     far_side = (-2, 2, 2)
 
-    def send_terms(arrays):
-        for array in arrays:
-            send_sums(0, array, block_sum(array, 4), far_side[array])
-            send_sums(1, array, block_sum(array, 3), 1)
-            send_sums(2, array, block_sum(array, -3), -1)
-        for array in arrays:
-            send_sums(3, array, block_sum(array, 1), 1)
-            send_sums(4, array, block_sum(array, -1), -1)
-
+    def send_terms(array):
+        send_sums(0, array, block_sum(array, 4), far_side[array])
+        send_sums(1, array, block_sum(array, 3), 1)
+        send_sums(2, array, block_sum(array, -3), -1)
+
+    def arrived_weights(j, dst):
+        loads[j].wait()
+        await_copy(dst, wsib_rs.at[j])
+
+    arrived_weights(0, sg)
+    arrived_weights(1, su)
     near, far = arrived_rows(0)
     acc[0] = dot(near, wg[...]) + dot(far, sg[...])
+    send_terms(0)
     acc[1] = dot(near, wu[...]) + dot(far, su[...])
-    send_terms((0, 1))
+    send_terms(1)
+    arrived_weights(2, sd)
     near, far = arrived_rows(1)
     acc[2] = dot_last(near, wd[...]) + dot_last(far, sd[...])
-    send_terms((2,))
+    send_terms(2)
+    for array in range(3):
+        send_sums(3, array, block_sum(array, 1), 1)
+        send_sums(4, array, block_sum(array, -1), -1)
     for array in range(3):
         for slot, hops in ((1, 2), (2, -2)):
             value = block_sum(array, hops) + received(slot, array)
@@ -214,7 +218,7 @@
     gate, up = swapped(0), swapped(1)
     sig = jax.nn.sigmoid(gate)
     hgu[own, 0] = (gate * sig * up).astype(BF16)
-    for lane, hops in enumerate((2, -2, 1, -1)):
+    for lane, hops in enumerate((2, -2)):
         spread(lane, 0, 0, hops)
     grad_hidden = swapped(2)
     hgu[own, 1] = (grad_hidden * up * sig * (1.0 + gate * (1.0 - sig))).astype(BF16)
@@ -223,7 +227,7 @@
     hgu[own, 2] = (grad_hidden * gate * sig).astype(BF16)
     for lane, hops in enumerate((2, -2)):
         spread(lane, 2, 0, hops)
-    for group in (1, 2):
+    for group in range(3):
         for lane, hops in ((2, 1), (3, -1)):
             spread(lane, group, 0, hops)
     for group in range(3):

time: 60.3 us -> 60 us (level)
  no operation moved by 1% of the time
where the time goes in v6:
time: 60 us; the launch traced here: 59.8 us
  Pallas kernels  59.2 us (99%)
  between operations  0.64 us (1%)
    pallas_call x1, Pallas kernels, on_device(): pl.pallas_call(kernel, out_shape=shapes, in_specs=[hbm] * 5, out_specs=[h...  57 us
    pallas_call x1, Pallas kernels, on_device(): pl.pallas_call(copy_out, out_shape=shapes, in_specs=[hbm] * 5, out_specs=...  2.21 us

profile of v6, /device:TPU:1, one launch (start us, length us, event | category | flops | bytes accessed | tf_op | source)
XLA Modules:
  0.0 59.8 jit_solution(7837671122268647500)
XLA Ops:
  0.6 57.0 %shard_map.92 = (bf16[16,256]{1,0:T(8,128)(2,1)}, bf16[16,256]{1,0:T(8,128)(2,1)}, bf16[256,896]{1,0:T(8,128)(2,1)}, bf16[256,896]{1,0:T(8,128)(2,1)}, bf16[896,256]{1,0:T(8,128)(2,1)}) custom-call(bf16[16,256]{1,0:T(8,128)(2,1)} %tok_hbm.1, bf16[16,256]{1,0:T(8,128)(2,1)} %cot_hbm.1, bf16[256,896]{1,0:T(8,128)(2,1)} %wg_hbm.1, bf16[256,896]{1,0:T(8,128)(2,1)} %wu_hbm.1, ...), custom_call_target="tpu_custom_call" | custom-call | tf_op jit(solution)/shard_map/pallas_call | solution.py:371
  57.6 2.2 %shard_map.93 = (bf16[16,256]{1,0:T(8,128)(2,1)}, bf16[16,256]{1,0:T(8,128)(2,1)}, bf16[256,896]{1,0:T(8,128)(2,1)}, bf16[256,896]{1,0:T(8,128)(2,1)}, bf16[896,256]{1,0:T(8,128)(2,1)}) custom-call(bf16[16,256]{1,0:T(8,128)(2,1)} %get-tuple-element.10.refs_0_, bf16[16,256]{1,0:T(8,128)(2,1)} %get-tuple-element.11.refs_1_, ...), custom_call_target="tpu_custom_call" | custom-call | tf_op jit(solution)/shard_map/pallas_call | solution.py:394

commit v7 on v6

--- a/solution.py
+++ b/solution.py
@@ -188,7 +188,6 @@
             if far_side[array] == hops:
                 value += received(0, array)
             send_sums(slot + 4, array, value, hops)
-    start(remote(rows.at[1 - core], other, oth_ss, oth_rs, sib))
     totals = []
     for array in range(3):
         total = block_sum(array, 0)
@@ -277,6 +276,7 @@
         arrive(5, group, -3)
         arrive(6, group, 4)
 
+    start(remote(rows.at[1 - core], other, oth_ss, oth_rs, sib))
     multiply_hidden((0, 1, -1, 2, -2))
     multiply_grads((0, 1, -1, 2, -2))
     arrive_far(0)

time: 60 us -> 60 us (level)
  no operation moved by 1% of the time
where the time goes in v7:
time: 60 us; the launch traced here: 59.8 us
  Pallas kernels  59.2 us (99%)
  between operations  0.64 us (1%)
    pallas_call x1, Pallas kernels, on_device(): pl.pallas_call(kernel, out_shape=shapes, in_specs=[hbm] * 5, out_specs=[h...  57 us
    pallas_call x1, Pallas kernels, on_device(): pl.pallas_call(copy_out, out_shape=shapes, in_specs=[hbm] * 5, out_specs=...  2.21 us

profile of v7, /device:TPU:1, one launch (start us, length us, event | category | flops | bytes accessed | tf_op | source)
XLA Modules:
  0.0 59.8 jit_solution(11763155260825159563)
XLA Ops:
  0.6 57.0 %shard_map.92 = (bf16[16,256]{1,0:T(8,128)(2,1)}, bf16[16,256]{1,0:T(8,128)(2,1)}, bf16[256,896]{1,0:T(8,128)(2,1)}, bf16[256,896]{1,0:T(8,128)(2,1)}, bf16[896,256]{1,0:T(8,128)(2,1)}) custom-call(bf16[16,256]{1,0:T(8,128)(2,1)} %tok_hbm.1, bf16[16,256]{1,0:T(8,128)(2,1)} %cot_hbm.1, bf16[256,896]{1,0:T(8,128)(2,1)} %wg_hbm.1, bf16[256,896]{1,0:T(8,128)(2,1)} %wu_hbm.1, ...), custom_call_target="tpu_custom_call" | custom-call | tf_op jit(solution)/shard_map/pallas_call | solution.py:371
  57.6 2.2 %shard_map.93 = (bf16[16,256]{1,0:T(8,128)(2,1)}, bf16[16,256]{1,0:T(8,128)(2,1)}, bf16[256,896]{1,0:T(8,128)(2,1)}, bf16[256,896]{1,0:T(8,128)(2,1)}, bf16[896,256]{1,0:T(8,128)(2,1)}) custom-call(bf16[16,256]{1,0:T(8,128)(2,1)} %get-tuple-element.10.refs_0_, bf16[16,256]{1,0:T(8,128)(2,1)} %get-tuple-element.11.refs_1_, ...), custom_call_target="tpu_custom_call" | custom-call | tf_op jit(solution)/shard_map/pallas_call | solution.py:394
